TPU v7x, 256 devices: a whole 4x4x8 slice. The times are simulated.
256 devices in a mesh: pts: 32 (over y, x, core), bas: 8 (over z).
Axes of the slice: x: 4, y: 4, z: 8, core: 2. Of those that a mesh axis runs over, the one named last changes fastest.
Arguments:
- chi: bfloat16 [128, 448, 2048], P('pts'), may hold values from -6 to 6
- dchi: bfloat16 [3, 128, 448, 2048], P(None, 'pts', None, 'bas'), may hold values from -6 to 6
- screen: int32 [128, 16], P('pts'), may hold values from 0 to 127, as said below
- density: bfloat16 [128, 128, 128, 128], P('pts', 'bas'), may hold values from -0.125 to 0.125
- weights: float32 [128, 448], P('pts'), may hold values from 0.002 to 0.02
- basis_atom: int32 [16384], P('bas'), may hold values from 0 to 3071, never falling along the last dimension, each value on 1 to 14 neighbouring positions
- neighbors: int32 [8, 57344], P(None, ('pts', 'bas')), may hold values from 0 to 3071
- weight_grad: float32 [3, 8, 57344], P(None, None, ('pts', 'bas')), may hold values from -0.046875 to 0.046875
Outputs:
- gradient: float32 [3, 3072], P(None, ('pts', 'bas'))
Inputs may be any that keep to these rules, and one draw needn't show every extreme that they name: `screen`: slot j of a box names a basis block k with k // 16 == j // 2. For a box on index q of pts, the slots with j // 2 == q // 4 name distinct blocks with k // 4 == q, and every other slot names a block with k // 4 != q. Among the 64 slots of the boxes of one index of pts, at most 8 name blocks with one value of k // 4, and at most 4 name blocks with one value of k // 4 other than that index.
All inputs are finite; a program needn't handle non-finite values.
Results may differ from a plain program's by a relative error of at most 0.0003.
Values may be sent and summed in bfloat16 or wider, within the bound.
No kernel may reach another device: no remote copies, remote signals or barrier semaphores. Data moves between devices by JAX's collectives and lax.ppermute only.
A program may use at most 192 MiB of HBM per device.

v0:
```python
import jax
import jax.numpy as jnp
from jax import lax
from jax.sharding import PartitionSpec as P

ATOMS = 3072


def request_rows(
    lists, requester, bas_index, owner_count, row_span, range_span, capacity, own_slots
):
    box_count, slot_count = lists.shape
    flat_ids = lists.reshape(-1)
    owner_of = flat_ids // row_span
    is_self = owner_of == requester
    sent = jnp.ones_like(is_self)
    onehot = jnp.logical_and(
        owner_of[:, None] == jnp.arange(owner_count, dtype=jnp.int32)[None, :], sent[:, None]
    ).astype(jnp.int32)
    before = jnp.cumsum(onehot, axis=0) - onehot
    slot_place = jnp.sum(before * onehot, axis=1)
    row_local = flat_ids - owner_of * row_span
    columns = (
        lax.dynamic_slice_in_dim(lists, bas_index * own_slots, own_slots, 1)
        - bas_index * range_span
    )
    columns = jnp.repeat(columns, slot_count, axis=0)
    record = jnp.concatenate([row_local[:, None], columns], axis=1)
    target = jnp.where(sent, owner_of, owner_count)
    empty_rows = jnp.zeros((owner_count, capacity, 1 + own_slots), jnp.int32)
    filled = empty_rows.at[target, slot_place].set(record, mode="drop")
    return (filled, owner_of, slot_place, is_self, record)


def look_up(density, record):
    return density[record[..., 0:1], record[..., 1:]]


def shards(chi, dchi, screen, density, weights, basis_atom, neighbors, weight_grad):
    box_count, box_pts, _ = chi.shape
    row_span, range_span, block_size, _ = density.shape
    n_pts = lax.axis_size("pts")
    n_bas = lax.axis_size("bas")
    slot_count = screen.shape[1]
    own_slots = slot_count // n_bas
    bas_index = lax.axis_index("bas")
    pts_index = lax.axis_index("pts")
    capacity = box_count * own_slots
    my_rows, owner_of, slot_place, is_self, my_record = request_rows(
        screen, pts_index, bas_index, n_pts, row_span, range_span, capacity, own_slots
    )
    blocks_found = look_up(
        density, lax.all_to_all(my_rows, "pts", split_axis=0, concat_axis=0, tiled=True)
    )
    arrived = lax.all_to_all(blocks_found, "pts", split_axis=0, concat_axis=0, tiled=True)
    place = jnp.minimum(slot_place, capacity - 1)
    fetched = arrived[owner_of, place]
    chosen = fetched.reshape(box_count, slot_count, own_slots, block_size, block_size)
    values = chi.reshape(box_count, box_pts, slot_count, block_size)
    fock_rows = jnp.einsum("xgsa,xsjac->xgjc", values, chosen, preferred_element_type=jnp.float32)
    fock_rows = fock_rows.reshape(box_count, box_pts, own_slots * block_size)
    own_values = lax.dynamic_slice_in_dim(
        chi, bas_index * own_slots * block_size, own_slots * block_size, 2
    )
    energy_part = jnp.sum(own_values.astype(jnp.float32) * fock_rows, axis=2).reshape(-1)
    energy = lax.psum_scatter(energy_part, "bas", scatter_dimension=0, tiled=True)
    basis_term = -2.0 * jnp.sum(
        weights[None, :, :, None] * dchi.astype(jnp.float32) * fock_rows[None], axis=2
    )
    own_list = (
        lax.dynamic_slice_in_dim(screen, bas_index * own_slots, own_slots, 1)
        - bas_index * range_span
    )
    functions = (
        own_list[:, :, None] * block_size + jnp.arange(block_size, dtype=jnp.int32)[None, None, :]
    ).reshape(box_count, -1)
    atom_ids = basis_atom[functions]
    gradient = jnp.zeros((3, ATOMS), jnp.float32)
    gradient = gradient.at[:, atom_ids.reshape(-1)].add(basis_term.reshape(3, -1))
    becke_terms = (energy[None, None, :] * weight_grad).reshape(3, -1)
    gradient = gradient.at[:, neighbors.reshape(-1)].add(becke_terms)
    return lax.psum_scatter(gradient, ("pts", "bas"), scatter_dimension=1, tiled=True)


def solution(mesh):
    in_specs = (
        P("pts", None, None),
        P(None, "pts", None, "bas"),
        P("pts", None),
        P("pts", "bas", None, None),
        P("pts", None),
        P("bas"),
        P(None, ("pts", "bas")),
        P(None, None, ("pts", "bas")),
    )
    out_specs = P(None, ("pts", "bas"))
    return jax.shard_map(shards, mesh=mesh, in_specs=in_specs, out_specs=out_specs, check_vma=False)
```

profile of v0, /device:TPU:1, one launch (start us, length us, event | category | flops | bytes accessed | tf_op | source)
XLA Modules:
  0.0 1476.5 jit_solution(15226440460039754584)
XLA Ops:
  7.0 15.7 %all_to_all.10 = s32[32,8,3]{1,2,0:T(4,128)S(1)} all-to-all(s32[32,8,3]{1,2,0:T(4,128)S(1)} %copy.24), channel_id=1, replica_groups=mesh['pts'=32,'bas'=8] {'pts'}, dimensions={0} | all-to-all | bytes 6144 | tf_op jit(solution)/shard_map/all_to_all | solution.py:53
  23.4 11.0 gather_fusion.1
  63.4 177.7 %all-to-all-done.1 = bf16[32,8,2,128,128]{4,3,2,1,0:T(8,128)(2,1)} async-done(((bf16[32,8,2,128,128]{4,3,2,1,0:T(8,128)(2,1)}), bf16[32,8,2,128,128]{4,3,2,1,0:T(8,128)(2,1)}, u32[]{:S(2)}, u32[]{:S(2)}) %all-to-all-start.1) | async-done | bytes 16777248 | tf_op jit(solution)/shard_map/all_to_all | solution.py:55
  262.9 16.6 %all-reduce = f32[1792]{0:T(1024)S(1)} all-reduce(f32[1792]{0:T(1024)S(1)} %reshape.295), channel_id=2, replica_groups=mesh['pts'=32,'bas'=8] {'bas'}, use_global_device_ids=true, to_apply=%region_6.7.clone | all-reduce | flops 1792 | bytes 14336
  289.2 13.1 scatter_fusion.1
  302.3 647.7 %fusion = f32[3,16]{0,1:T(8,128)S(1)} fusion(f32[3,3072]{0,1:T(8,128)} %scatter_fusion.1), kind=kCustom, calls=%all-reduce-scatter | all-reduce-scatter fusion | flops 12289 | bytes 37056
  950.0 20.6 %collective-permute-start = (f32[3,16]{0,1:T(8,128)S(1)}, f32[3,16]{0,1:T(8,128)S(1)}, u32[]{:S(2)}, u32[]{:S(2)}) collective-permute-start(f32[3,16]{0,1:T(8,128)S(1)} %fusion), channel_id=1, source_target_pairs={{0,1},{1,2},{2,3},{3,4},{4,5},{5,6},{6,7},{7,8},{8,9},{9,10},{10,1... | collective-permute-start | bytes 584
  970.6 13.1 collective-permute-start.1
  987.1 13.0 collective-permute-start.10
  1000.0 13.1 collective-permute-start.11
  1013.2 13.1 collective-permute-start.12
  1026.3 13.1 collective-permute-start.13
  1039.5 13.1 collective-permute-start.14
  1052.6 13.1 collective-permute-start.15
  1065.7 13.1 collective-permute-start.16
  1078.9 13.1 collective-permute-start.17
  1092.0 13.1 collective-permute-start.18
  1105.2 13.1 collective-permute-start.19
  1118.3 13.1 collective-permute-start.2
  1131.5 13.1 collective-permute-start.20
  1144.6 13.1 collective-permute-start.21
  1157.7 13.1 collective-permute-start.22
  1170.9 13.1 collective-permute-start.23
  1184.0 13.1 collective-permute-start.24
  1197.1 13.1 collective-permute-start.25
  1210.3 13.1 collective-permute-start.26
  1223.4 13.1 collective-permute-start.27
  1236.6 13.1 collective-permute-start.28
  1249.7 13.1 collective-permute-start.29
  1262.8 13.1 collective-permute-start.3
  1441.8 13.1 collective-permute-start.8
  1454.9 13.1 collective-permute-start.9
  (174 shorter events, 244.2 us)
Async XLA Ops:
  34.4 206.7 %all-to-all-start.1 = ((bf16[32,8,2,128,128]{4,3,2,1,0:T(8,128)(2,1)}), bf16[32,8,2,128,128]{4,3,2,1,0:T(8,128)(2,1)}, u32[]{:S(2)}, u32[]{:S(2)}) async-start(bf16[32,8,2,128,128]{4,3,2,1,0:T(8,128)(2,1)} %bitcast.61), calls=%async_computation.1 | async-start | bytes 33554432 | tf_op jit(solution)/shard_map/all_to_all | solution.py:55
  950.0 76.3 %collective-permute-start = (f32[3,16]{0,1:T(8,128)S(1)}, f32[3,16]{0,1:T(8,128)S(1)}, u32[]{:S(2)}, u32[]{:S(2)}) collective-permute-start(f32[3,16]{0,1:T(8,128)S(1)} %fusion), channel_id=1, source_target_pairs={{0,1},{1,2},{2,3},{3,4},{4,5},{5,6},{6,7},{7,8},{8,9},{9,10},{10,1... | collective-permute-start | bytes 584
  970.6 68.8 %collective-permute-start.1 = (f32[3,16]{0,1:T(8,128)S(1)}, f32[3,16]{0,1:T(8,128)S(1)}, u32[]{:S(2)}, u32[]{:S(2)}) collective-permute-start(f32[3,16]{0,1:T(8,128)S(1)} %fusion), channel_id=1, source_target_pairs={{0,2},{1,3},{2,4},{3,5},{4,6},{5,7},{6,8},{7,9},{8,10},{9,11},{10,... | collective-permute-start | bytes 584
  987.1 65.5 %collective-permute-start.10 = (f32[3,16]{0,1:T(8,128)S(1)}, f32[3,16]{0,1:T(8,128)S(1)}, u32[]{:S(2)}, u32[]{:S(2)}) collective-permute-start(f32[3,16]{0,1:T(8,128)S(1)} %fusion), channel_id=1, source_target_pairs={{0,11},{1,12},{2,13},{3,14},{4,15},{5,16},{6,17},{7,18},{8,19},{9,... | collective-permute-start | bytes 584
  1000.0 65.7 %collective-permute-start.11 = (f32[3,16]{0,1:T(8,128)S(1)}, f32[3,16]{0,1:T(8,128)S(1)}, u32[]{:S(2)}, u32[]{:S(2)}) collective-permute-start(f32[3,16]{0,1:T(8,128)S(1)} %fusion), channel_id=1, source_target_pairs={{0,12},{1,13},{2,14},{3,15},{4,16},{5,17},{6,18},{7,19},{8,20},{9,... | collective-permute-start | bytes 584
  1013.2 65.7 %collective-permute-start.12 = (f32[3,16]{0,1:T(8,128)S(1)}, f32[3,16]{0,1:T(8,128)S(1)}, u32[]{:S(2)}, u32[]{:S(2)}) collective-permute-start(f32[3,16]{0,1:T(8,128)S(1)} %fusion), channel_id=1, source_target_pairs={{0,13},{1,14},{2,15},{3,16},{4,17},{5,18},{6,19},{7,20},{8,21},{9,... | collective-permute-start | bytes 584
  1026.3 65.7 %collective-permute-start.13 = (f32[3,16]{0,1:T(8,128)S(1)}, f32[3,16]{0,1:T(8,128)S(1)}, u32[]{:S(2)}, u32[]{:S(2)}) collective-permute-start(f32[3,16]{0,1:T(8,128)S(1)} %fusion), channel_id=1, source_target_pairs={{0,14},{1,15},{2,16},{3,17},{4,18},{5,19},{6,20},{7,21},{8,22},{9,... | collective-permute-start | bytes 584
  1039.5 65.7 %collective-permute-start.14 = (f32[3,16]{0,1:T(8,128)S(1)}, f32[3,16]{0,1:T(8,128)S(1)}, u32[]{:S(2)}, u32[]{:S(2)}) collective-permute-start(f32[3,16]{0,1:T(8,128)S(1)} %fusion), channel_id=1, source_target_pairs={{0,15},{1,16},{2,17},{3,18},{4,19},{5,20},{6,21},{7,22},{8,23},{9,... | collective-permute-start | bytes 584
  1052.6 65.7 %collective-permute-start.15 = (f32[3,16]{0,1:T(8,128)S(1)}, f32[3,16]{0,1:T(8,128)S(1)}, u32[]{:S(2)}, u32[]{:S(2)}) collective-permute-start(f32[3,16]{0,1:T(8,128)S(1)} %fusion), channel_id=1, source_target_pairs={{0,16},{1,17},{2,18},{3,19},{4,20},{5,21},{6,22},{7,23},{8,24},{9,... | collective-permute-start | bytes 584
  1065.7 65.7 %collective-permute-start.16 = (f32[3,16]{0,1:T(8,128)S(1)}, f32[3,16]{0,1:T(8,128)S(1)}, u32[]{:S(2)}, u32[]{:S(2)}) collective-permute-start(f32[3,16]{0,1:T(8,128)S(1)} %fusion), channel_id=1, source_target_pairs={{0,17},{1,18},{2,19},{3,20},{4,21},{5,22},{6,23},{7,24},{8,25},{9,... | collective-permute-start | bytes 584
  1078.9 65.7 %collective-permute-start.17 = (f32[3,16]{0,1:T(8,128)S(1)}, f32[3,16]{0,1:T(8,128)S(1)}, u32[]{:S(2)}, u32[]{:S(2)}) collective-permute-start(f32[3,16]{0,1:T(8,128)S(1)} %fusion), channel_id=1, source_target_pairs={{0,18},{1,19},{2,20},{3,21},{4,22},{5,23},{6,24},{7,25},{8,26},{9,... | collective-permute-start | bytes 584
  1092.0 65.7 %collective-permute-start.18 = (f32[3,16]{0,1:T(8,128)S(1)}, f32[3,16]{0,1:T(8,128)S(1)}, u32[]{:S(2)}, u32[]{:S(2)}) collective-permute-start(f32[3,16]{0,1:T(8,128)S(1)} %fusion), channel_id=1, source_target_pairs={{0,19},{1,20},{2,21},{3,22},{4,23},{5,24},{6,25},{7,26},{8,27},{9,... | collective-permute-start | bytes 584
  1105.2 65.7 %collective-permute-start.19 = (f32[3,16]{0,1:T(8,128)S(1)}, f32[3,16]{0,1:T(8,128)S(1)}, u32[]{:S(2)}, u32[]{:S(2)}) collective-permute-start(f32[3,16]{0,1:T(8,128)S(1)} %fusion), channel_id=1, source_target_pairs={{0,20},{1,21},{2,22},{3,23},{4,24},{5,25},{6,26},{7,27},{8,28},{9,... | collective-permute-start | bytes 584
  1118.3 65.7 %collective-permute-start.2 = (f32[3,16]{0,1:T(8,128)S(1)}, f32[3,16]{0,1:T(8,128)S(1)}, u32[]{:S(2)}, u32[]{:S(2)}) collective-permute-start(f32[3,16]{0,1:T(8,128)S(1)} %fusion), channel_id=1, source_target_pairs={{0,3},{1,4},{2,5},{3,6},{4,7},{5,8},{6,9},{7,10},{8,11},{9,12},{10... | collective-permute-start | bytes 584
  1131.5 65.7 %collective-permute-start.20 = (f32[3,16]{0,1:T(8,128)S(1)}, f32[3,16]{0,1:T(8,128)S(1)}, u32[]{:S(2)}, u32[]{:S(2)}) collective-permute-start(f32[3,16]{0,1:T(8,128)S(1)} %fusion), channel_id=1, source_target_pairs={{0,21},{1,22},{2,23},{3,24},{4,25},{5,26},{6,27},{7,28},{8,29},{9,... | collective-permute-start | bytes 584
  1144.6 65.7 %collective-permute-start.21 = (f32[3,16]{0,1:T(8,128)S(1)}, f32[3,16]{0,1:T(8,128)S(1)}, u32[]{:S(2)}, u32[]{:S(2)}) collective-permute-start(f32[3,16]{0,1:T(8,128)S(1)} %fusion), channel_id=1, source_target_pairs={{0,22},{1,23},{2,24},{3,25},{4,26},{5,27},{6,28},{7,29},{8,30},{9,... | collective-permute-start | bytes 584
  1157.7 65.7 %collective-permute-start.22 = (f32[3,16]{0,1:T(8,128)S(1)}, f32[3,16]{0,1:T(8,128)S(1)}, u32[]{:S(2)}, u32[]{:S(2)}) collective-permute-start(f32[3,16]{0,1:T(8,128)S(1)} %fusion), channel_id=1, source_target_pairs={{0,23},{1,24},{2,25},{3,26},{4,27},{5,28},{6,29},{7,30},{8,31},{9,... | collective-permute-start | bytes 584
  1170.9 65.7 %collective-permute-start.23 = (f32[3,16]{0,1:T(8,128)S(1)}, f32[3,16]{0,1:T(8,128)S(1)}, u32[]{:S(2)}, u32[]{:S(2)}) collective-permute-start(f32[3,16]{0,1:T(8,128)S(1)} %fusion), channel_id=1, source_target_pairs={{0,24},{1,25},{2,26},{3,27},{4,28},{5,29},{6,30},{7,31},{8,32},{9,... | collective-permute-start | bytes 584
  1184.0 65.7 %collective-permute-start.24 = (f32[3,16]{0,1:T(8,128)S(1)}, f32[3,16]{0,1:T(8,128)S(1)}, u32[]{:S(2)}, u32[]{:S(2)}) collective-permute-start(f32[3,16]{0,1:T(8,128)S(1)} %fusion), channel_id=1, source_target_pairs={{0,25},{1,26},{2,27},{3,28},{4,29},{5,30},{6,31},{7,32},{8,33},{9,... | collective-permute-start | bytes 584
  1197.1 65.7 %collective-permute-start.25 = (f32[3,16]{0,1:T(8,128)S(1)}, f32[3,16]{0,1:T(8,128)S(1)}, u32[]{:S(2)}, u32[]{:S(2)}) collective-permute-start(f32[3,16]{0,1:T(8,128)S(1)} %fusion), channel_id=1, source_target_pairs={{0,26},{1,27},{2,28},{3,29},{4,30},{5,31},{6,32},{7,33},{8,34},{9,... | collective-permute-start | bytes 584
  1210.3 65.7 %collective-permute-start.26 = (f32[3,16]{0,1:T(8,128)S(1)}, f32[3,16]{0,1:T(8,128)S(1)}, u32[]{:S(2)}, u32[]{:S(2)}) collective-permute-start(f32[3,16]{0,1:T(8,128)S(1)} %fusion), channel_id=1, source_target_pairs={{0,27},{1,28},{2,29},{3,30},{4,31},{5,32},{6,33},{7,34},{8,35},{9,... | collective-permute-start | bytes 584
  1223.4 61.5 %collective-permute-start.27 = (f32[3,16]{0,1:T(8,128)S(1)}, f32[3,16]{0,1:T(8,128)S(1)}, u32[]{:S(2)}, u32[]{:S(2)}) collective-permute-start(f32[3,16]{0,1:T(8,128)S(1)} %fusion), channel_id=1, source_target_pairs={{0,28},{1,29},{2,30},{3,31},{4,32},{5,33},{6,34},{7,35},{8,36},{9,... | collective-permute-start | bytes 584
  1236.6 51.5 %collective-permute-start.28 = (f32[3,16]{0,1:T(8,128)S(1)}, f32[3,16]{0,1:T(8,128)S(1)}, u32[]{:S(2)}, u32[]{:S(2)}) collective-permute-start(f32[3,16]{0,1:T(8,128)S(1)} %fusion), channel_id=1, source_target_pairs={{0,29},{1,30},{2,31},{3,32},{4,33},{5,34},{6,35},{7,36},{8,37},{9,... | collective-permute-start | bytes 584
  1249.7 39.7 %collective-permute-start.29 = (f32[3,16]{0,1:T(8,128)S(1)}, f32[3,16]{0,1:T(8,128)S(1)}, u32[]{:S(2)}, u32[]{:S(2)}) collective-permute-start(f32[3,16]{0,1:T(8,128)S(1)} %fusion), channel_id=1, source_target_pairs={{0,30},{1,31},{2,32},{3,33},{4,34},{5,35},{6,36},{7,37},{8,38},{9,... | collective-permute-start | bytes 584
  1262.8 32.0 %collective-permute-start.3 = (f32[3,16]{0,1:T(8,128)S(1)}, f32[3,16]{0,1:T(8,128)S(1)}, u32[]{:S(2)}, u32[]{:S(2)}) collective-permute-start(f32[3,16]{0,1:T(8,128)S(1)} %fusion), channel_id=1, source_target_pairs={{0,4},{1,5},{2,6},{3,7},{4,8},{5,9},{6,10},{7,11},{8,12},{9,13},{1... | collective-permute-start | bytes 584
  1326.8 30.6 %collective-permute-start.40 = (f32[3,16]{0,1:T(8,128)S(1)}, f32[3,16]{0,1:T(8,128)S(1)}, u32[]{:S(2)}, u32[]{:S(2)}) collective-permute-start(f32[3,16]{0,1:T(8,128)S(1)} %fusion), channel_id=1, source_target_pairs={{0,41},{1,42},{2,43},{3,44},{4,45},{5,46},{6,47},{7,48},{8,49},{9,... | collective-permute-start | bytes 584
  1366.0 31.1 %collective-permute-start.5 = (f32[3,16]{0,1:T(8,128)S(1)}, f32[3,16]{0,1:T(8,128)S(1)}, u32[]{:S(2)}, u32[]{:S(2)}) collective-permute-start(f32[3,16]{0,1:T(8,128)S(1)} %fusion), channel_id=1, source_target_pairs={{0,6},{1,7},{2,8},{3,9},{4,10},{5,11},{6,12},{7,13},{8,14},{9,15},... | collective-permute-start | bytes 584
  1411.2 30.6 %collective-permute-start.6 = (f32[3,16]{0,1:T(8,128)S(1)}, f32[3,16]{0,1:T(8,128)S(1)}, u32[]{:S(2)}, u32[]{:S(2)}) collective-permute-start(f32[3,16]{0,1:T(8,128)S(1)} %fusion), channel_id=1, source_target_pairs={{0,7},{1,8},{2,9},{3,10},{4,11},{5,12},{6,13},{7,14},{8,15},{9,16}... | collective-permute-start | bytes 584
  1417.8 37.1 %collective-permute-start.60 = (f32[3,16]{0,1:T(8,128)S(1)}, f32[3,16]{0,1:T(8,128)S(1)}, u32[]{:S(2)}, u32[]{:S(2)}) collective-permute-start(f32[3,16]{0,1:T(8,128)S(1)} %fusion), channel_id=1, source_target_pairs={{0,61},{1,62},{2,63},{3,64},{4,65},{5,66},{6,67},{7,68},{8,69},{9,... | collective-permute-start | bytes 584
  1426.5 41.5 %collective-permute-start.61 = (f32[3,16]{0,1:T(8,128)S(1)}, f32[3,16]{0,1:T(8,128)S(1)}, u32[]{:S(2)}, u32[]{:S(2)}) collective-permute-start(f32[3,16]{0,1:T(8,128)S(1)} %fusion), channel_id=1, source_target_pairs={{0,62},{1,63},{2,64},{3,65},{4,66},{5,67},{6,68},{7,69},{8,70},{9,... | collective-permute-start | bytes 584
  1430.3 37.7 %collective-permute-start.62 = (f32[3,16]{0,1:T(8,128)S(1)}, f32[3,16]{0,1:T(8,128)S(1)}, u32[]{:S(2)}, u32[]{:S(2)}) collective-permute-start(f32[3,16]{0,1:T(8,128)S(1)} %fusion), channel_id=1, source_target_pairs={{0,63},{1,64},{2,65},{3,66},{4,67},{5,68},{6,69},{7,70},{8,71},{9,... | collective-permute-start | bytes 584
  1433.2 34.8 %collective-permute-start.7 = (f32[3,16]{0,1:T(8,128)S(1)}, f32[3,16]{0,1:T(8,128)S(1)}, u32[]{:S(2)}, u32[]{:S(2)}) collective-permute-start(f32[3,16]{0,1:T(8,128)S(1)} %fusion), channel_id=1, source_target_pairs={{0,8},{1,9},{2,10},{3,11},{4,12},{5,13},{6,14},{7,15},{8,16},{9,17... | collective-permute-start | bytes 584
  (42 other events, 1990.4 us)
where the time goes:
time: 1490 us; the launch traced here: 1480 us
  blocking collectives  680 us (46%)
  starting transfers between devices  522 us (35%)
  waiting for transfers between devices  179 us (12%)
  local copies, waits for them, and re-layouts  61.4 us (4%)
  other arithmetic  26 us (2%)
    unnamed x2, blocking collectives  664 us
    unnamed x64, starting transfers between devices  517 us
    all_to_all x1, waiting for transfers between devices, shards(): lax.all_to_all(blocks_found, 'pts', split_axis=0, concat_axis=0, tiled=True)  178 us
  transfers between devices with their start and end apart: 65, of which 2 were waited for; matrix products, arithmetic and copies ran while one was open for 2% of the time, Pallas kernels for 0%

commit v1 on v0

v1 whole, which is shorter than its diff:
```python
import jax
import jax.numpy as jnp
from jax import lax
from jax.sharding import PartitionSpec as P

ATOMS = 3072
CAPACITY = 4


def ranks_of(owner, valid):
    same = jnp.logical_and(owner[..., :, None] == owner[..., None, :], valid[..., None, :])
    count = owner.shape[-1]
    earlier = jnp.arange(count)[None, :] < jnp.arange(count)[:, None]
    return jnp.sum(jnp.logical_and(same, earlier).astype(jnp.int32), axis=-1)


def shards(chi, dchi, screen, density, weights, basis_atom, neighbors, weight_grad):
    box_count, box_pts, _ = chi.shape
    row_span, range_span, block_size, _ = density.shape
    n_pts = lax.axis_size("pts")
    n_bas = lax.axis_size("bas")
    slot_count = screen.shape[1]
    own_slots = slot_count // n_bas
    bas_index = lax.axis_index("bas")
    pts_index = lax.axis_index("pts")
    group = n_pts // n_bas
    home = pts_index // group
    flat = jnp.broadcast_to(screen.reshape(1, 1, -1), (n_pts, 1, box_count * slot_count))
    lists = lax.all_to_all(flat, "pts", split_axis=0, concat_axis=0, tiled=True)
    lists = lists.reshape(n_pts, box_count, slot_count)
    asked = lax.dynamic_slice_in_dim(lists, home * own_slots, own_slots, 2).reshape(n_pts, -1)
    columns = lax.dynamic_slice_in_dim(lists, bas_index * own_slots, own_slots, 2) - bas_index * range_span
    mine = asked // row_span == pts_index
    rank = ranks_of(asked // row_span, mine)
    place = jnp.arange(CAPACITY, dtype=jnp.int32)
    picked = jnp.logical_and(mine[:, None, :], rank[:, None, :] == place[None, :, None]).astype(jnp.int32)
    send_row = jnp.sum(picked * (asked % row_span)[:, None, :], axis=-1)
    entry_columns = jnp.repeat(columns, own_slots, axis=1)
    send_columns = jnp.sum(picked[..., None] * entry_columns[:, None], axis=2)
    outgoing = density[send_row[..., None], send_columns]
    arrived = lax.all_to_all(outgoing, "pts", split_axis=0, concat_axis=0, tiled=True)
    own_lists = screen.reshape(box_count, n_bas, own_slots).transpose(1, 0, 2).reshape(n_bas, -1)
    own_owner = own_lists // row_span
    own_place = jnp.minimum(ranks_of(own_owner, own_owner >= 0), CAPACITY - 1)
    index = own_owner * CAPACITY + own_place
    index = index.reshape(n_bas, box_count, own_slots).transpose(1, 0, 2).reshape(-1)
    fetched = arrived.reshape(n_pts * CAPACITY, own_slots, block_size, block_size)[index]
    fetched = fetched.reshape(box_count, slot_count, own_slots, block_size, block_size)
    own_columns = lax.dynamic_slice_in_dim(screen, bas_index * own_slots, own_slots, 1) - bas_index * range_span
    home_rows = lax.dynamic_slice_in_dim(screen, home * own_slots, own_slots, 1) - pts_index * row_span
    local = density[home_rows[:, :, None], own_columns[:, None, :]]
    chosen = lax.dynamic_update_slice_in_dim(fetched, local, home * own_slots, 1)
    values = chi.reshape(box_count, box_pts, slot_count, block_size)
    fock_rows = jnp.einsum("xgsa,xsjac->xgjc", values, chosen, preferred_element_type=jnp.float32)
    fock_rows = fock_rows.reshape(box_count, box_pts, own_slots * block_size)
    own_values = lax.dynamic_slice_in_dim(
        chi, bas_index * own_slots * block_size, own_slots * block_size, 2
    )
    energy_part = jnp.sum(own_values.astype(jnp.float32) * fock_rows, axis=2).reshape(n_bas, 1, -1)
    energy = jnp.sum(lax.all_to_all(energy_part, "bas", split_axis=0, concat_axis=0, tiled=True), axis=(0, 1))
    basis_term = -2.0 * jnp.sum(
        weights[None, :, :, None] * dchi.astype(jnp.float32) * fock_rows[None], axis=2
    )
    functions = (
        own_columns[:, :, None] * block_size + jnp.arange(block_size, dtype=jnp.int32)[None, None, :]
    ).reshape(box_count, -1)
    atom_ids = basis_atom[functions]
    gradient = jnp.zeros((3, ATOMS), jnp.float32)
    gradient = gradient.at[:, atom_ids.reshape(-1)].add(basis_term.reshape(3, -1))
    becke_terms = (energy[None, None, :] * weight_grad).reshape(3, -1)
    gradient = gradient.at[:, neighbors.reshape(-1)].add(becke_terms)
    devices = n_pts * n_bas
    parts = gradient.reshape(3, devices, -1).transpose(1, 0, 2).reshape(devices, 1, -1)
    parts = lax.all_to_all(parts, ("pts", "bas"), split_axis=0, concat_axis=0, tiled=True)
    return jnp.sum(parts, axis=(0, 1)).reshape(3, -1)


def solution(mesh):
    in_specs = (
        P("pts", None, None),
        P(None, "pts", None, "bas"),
        P("pts", None),
        P("pts", "bas", None, None),
        P("pts", None),
        P("bas"),
        P(None, ("pts", "bas")),
        P(None, None, ("pts", "bas")),
    )
    out_specs = P(None, ("pts", "bas"))
    return jax.shard_map(shards, mesh=mesh, in_specs=in_specs, out_specs=out_specs, check_vma=False)
```

time: 1490 us -> 215 us (0.14)
  blocking collectives: 680 us -> 27.8 us
  starting transfers between devices: 522 us -> 22.2 us
  waiting for transfers between devices: 179 us -> 81.6 us
    unnamed x2 -> x0, blocking collectives: 664 us -> none
    unnamed x64 -> x0, starting transfers between devices: 517 us -> none
    all_to_all x1 -> x3, waiting for transfers between devices: 178 us -> 81.6 us  [the longest x1 75.6 us: shards(): lax.all_to_all(outgoing, 'pts', split_axis=0, concat_axis=0, tiled=True)]
    all_to_all x1 -> x3, starting transfers between devices: 5.15 us -> 22.2 us  [the longest x1 8.59 us: shards(): lists = lax.all_to_all(flat, 'pts', split_axis=0, concat_axis=0, tiled=True)]
  transfers between devices with their start and end apart: 65 -> 3, of which waited for: 2 -> 2; matrix products, arithmetic and copies ran while one was open for 2% -> 17% of each run, Pallas kernels for 0% -> 0%
where the time goes in v1:
time: 215 us
  waiting for transfers between devices  81.6 us (38%)
  local copies, waits for them, and re-layouts  49.4 us (23%)
  blocking collectives  27.8 us (13%)
  other arithmetic  26.8 us (12%)
  starting transfers between devices  22.2 us (10%)
  matrix products  6.54 us (3%)
    all_to_all x1, waiting for transfers between devices, shards(): lax.all_to_all(outgoing, 'pts', split_axis=0, concat_axis=0, tiled=True)  75.6 us
    all_to_all x1, blocking collectives, shards(): lax.all_to_all(parts, ('pts', 'bas'), split_axis=0, concat_axis=0, tiled=...  27.8 us
    scatter-add x1, other arithmetic, shards(): gradient = gradient.at[:, neighbors.reshape(-1)].add(becke_terms)  13.1 us
    gather x1, local copies, waits for them, and re-layouts, shards(): outgoing = density[send_row[..., None], send_columns]  9.77 us
    unnamed x15, local copies, waits for them, and re-layouts  9.67 us
    all_to_all x1, starting transfers between devices, shards(): lists = lax.all_to_all(flat, 'pts', split_axis=0, concat_axis=0, tiled=True)  8.59 us
    all_to_all x1, starting transfers between devices, shards(): lax.all_to_all(energy_part, 'bas', split_axis=0, concat_axis=0, tiled=True)  8.21 us
    scatter-add x1, other arithmetic, shards(): gradient.at[:, atom_ids.reshape(-1)].add(basis_term.reshape(3, -1))  7.93 us
  transfers between devices with their start and end apart: 3, of which 2 were waited for; matrix products, arithmetic and copies ran while one was open for 17% of the time, Pallas kernels for 0%

profile of v1, /device:TPU:1, one launch (start us, length us, event | category | flops | bytes accessed | tf_op | source)
XLA Modules:
  0.0 214.5 jit_solution(16218389244736868437)
XLA Ops:
  0.0 0.9 broadcast_in_dim.15
  0.9 0.6 broadcast_in_dim.16
  1.5 8.6 %all-to-all-start = ((s32[32,1,64]{2,1,0:T(1,128)}), s32[32,1,64]{2,1,0:T(1,128)S(1)}, u32[]{:S(2)}, u32[]{:S(2)}) async-start(s32[32,1,64]{2,1,0:T(1,128)} %broadcast_in_dim.16), calls=%async_computation | async-start | bytes 32768 | tf_op jit(solution)/shard_map/all_to_all | solution.py:29
  10.1 0.8 copy.87
  11.1 6.0 %all-to-all-done = s32[32,1,64]{2,1,0:T(1,128)S(1)} async-done(((s32[32,1,64]{2,1,0:T(1,128)}), s32[32,1,64]{2,1,0:T(1,128)S(1)}, u32[]{:S(2)}, u32[]{:S(2)}) %all-to-all-start) | async-done | bytes 8224 | tf_op jit(solution)/shard_map/all_to_all | solution.py:29
  17.5 0.1 reshape.429
  17.7 9.8 %gather_fusion.1 = bf16[256,128,128]{2,1,0:T(8,128)(2,1)} fusion(bf16[4,16,128,128]{3,2,1,0:T(8,128)(2,1)S(1)} %copy-done, s32[256]{0:T(256)S(1)} %reshape.429), kind=kCustom, calls=%fused_computation.1 | custom fusion | bytes 16779264 | tf_op jit(solution)/shard_map/gather | solution.py:40
  27.4 5.4 %all-to-all-start.1 = ((bf16[32,4,2,128,128]{4,3,2,1,0:T(8,128)(2,1)}), bf16[32,4,2,128,128]{4,3,2,1,0:T(8,128)(2,1)}, u32[]{:S(2)}, u32[]{:S(2)}) async-start(bf16[32,4,2,128,128]{4,3,2,1,0:T(8,128)(2,1)} %bitcast.58), calls=%async_computation.1 | async-start | bytes 16777216 | tf_op jit(solution)/shard_map/all_to_all | solution.py:41
  32.8 0.3 convert_reduce_fusion
  33.7 0.7 gather_fusion.3
  34.4 8.9 %copy.114 = bf16[224,8,16,128]{3,2,1,0:T(8,128)(2,1)} copy(bf16[224,8,16,128]{3,1,2,0:T(8,128)(2,1)} %bitcast.60) | data formatting | bytes 14680064
  43.5 6.2 %gather_fusion = s32[1024]{0:T(1024)S(1)} fusion(s32[2048]{0:T(1024)S(1)} %copy-done.1, s32[1024]{0:T(1024)S(1)} %broadcast_clamp_fusion), kind=kCustom, calls=%fused_computation | custom fusion | bytes 12288 | tf_op jit(solution)/shard_map/gather | solution.py:67
  49.7 7.3 %bitcast_bitcast_fusion = bf16[4,448,16,128,1]{3,2,1,0,4:T(8,128)(2,1)} fusion(bf16[4,448,16,128]{3,2,1,0:T(8,128)(2,1)} %bitcast.59), kind=kLoop, calls=%fused_computation.6 | loop fusion | bytes 14680064 | tf_op jit(solution)/shard_map/reshape | solution.py:53
  57.0 75.6 %all-to-all-done.1 = bf16[32,4,2,128,128]{4,3,2,1,0:T(8,128)(2,1)} async-done(((bf16[32,4,2,128,128]{4,3,2,1,0:T(8,128)(2,1)}), bf16[32,4,2,128,128]{4,3,2,1,0:T(8,128)(2,1)}, u32[]{:S(2)}, u32[]{:S(2)}) %all-to-all-start.1) | async-done | bytes 8388640 | tf_op jit(solution)/shard_map/all_to_all | solution.py:41
  132.6 6.4 %gather_fusion.2 = bf16[64,2,128,128]{3,2,1,0:T(8,128)(2,1)} fusion(bf16[128,2,128,128]{3,2,1,0:T(8,128)(2,1)} %bitcast.8, s32[1024]{0:T(1024)S(1)} %pad_clamp_fusion), kind=kCustom, calls=%fused_computation.2 | custom fusion | bytes 8388864 | tf_op jit(solution)/shard_map/gather | solution.py:47
  139.1 0.9 constant_dynamic-update-slice_fusion
  139.9 6.5 %fusion.3 = f32[4,2,56,8,128]{4,3,2,1,0:T(8,128)S(1)} fusion(bf16[4,16,2,128,128]{4,3,2,1,0:T(8,128)(2,1)} %constant_dynamic-update-slice_fusion, bf16[4,448,16,128,1]{3,2,1,0,4:T(8,128)(2,1)} %bitcast_bitcast_fusion), kind=kOutput, calls=%fused_computation.13 | convolution fusion | flops 1879048192 | bytes 13369344 | tf_op jit(solution)/shard_map/xgsa,xsjac->xgjc/dot_general | solution.py:54
  146.5 1.4 copy.129
  147.9 1.6 multiply_reduce_fusion.1
  149.5 0.7 reshape.416
  150.2 8.2 %all-to-all-start.2 = ((f32[8,1,224]{2,1,0:T(1,128)}), f32[8,1,224]{2,1,0:T(1,128)S(1)}, u32[]{:S(2)}, u32[]{:S(2)}) async-start(f32[8,1,224]{2,1,0:T(1,128)} %reshape.416), calls=%async_computation.2 | async-start | bytes 16384 | tf_op jit(solution)/shard_map/all_to_all | solution.py:60
  158.4 3.1 %multiply_reduce_fusion = f32[3,4,256]{2,1,0:T(4,128)S(1)} fusion(bf16[3,4,448,256]{3,2,1,0:T(8,128)(2,1)} %param.9, f32[4,448,256]{2,1,0:T(8,128)} %bitcast.61, f32[4,448]{1,0:T(4,128)S(1)} %copy-done.4), kind=kLoop, calls=%fused_computation.9 | loop fusion | flops 5501952 | bytes 4606976 | tf_op jit(solution)/shard_map/reduce_sum | solution.py:61
  161.5 0.2 copy.109
  161.8 7.9 %scatter_custom_fusion = f32[3,3072]{0,1:T(8,128)} fusion(s32[1024]{0:T(1024)S(1)} %bitcast.77, f32[1024,3]{1,0:T(8,128)S(1)} %bitcast.66, f32[]{:T(128)} %constant.41.clone.1), kind=kCustom, calls=%fused_computation.14 | custom fusion | flops 3072 | bytes 36868 | tf_op jit(solution)/shard_map/scatter-add | solution.py:69
  169.7 0.3 copy.110
  170.1 13.1 %scatter_fusion = f32[3,3072]{0,1:T(8,128)} fusion(f32[3,3072]{0,1:T(8,128)} %scatter_custom_fusion, s32[1792]{0:T(1024)S(1)} %fusion.12, f32[1792,3]{1,0:T(8,128)S(1)} %bitcast.65), kind=kCustom, calls=%fused_computation.5 | custom fusion | flops 5376 | bytes 71680 | tf_op jit(solution)/shard_map/scatter-add | solution.py:71
  183.2 1.9 copy.102
  185.1 0.4 reshape.418
  185.5 0.2 copy.103
  185.8 27.8 %all_to_all.20 = f32[256,1,36]{2,1,0:T(1,128)S(1)} all-to-all(f32[256,1,36]{2,1,0:T(1,128)S(1)} %copy.104), channel_id=1, replica_groups=mesh['pts'=32,'bas'=8] {'pts','bas'}, dimensions={0} | all-to-all | bytes 73728 | tf_op jit(solution)/shard_map/all_to_all | solution.py:74
  213.6 0.3 reduce_sum.82
  213.8 0.7 reshape.420
  (54 shorter events, 1.5 us)
Async XLA Ops:
  0.0 17.7 %copy-start = (bf16[4,16,128,128]{3,2,1,0:T(8,128)(2,1)S(1)}, bf16[4,16,128,128]{3,2,1,0:T(8,128)(2,1)}, u32[]{:S(2)}) copy-start(bf16[4,16,128,128]{3,2,1,0:T(8,128)(2,1)} %param.11) | copy-start | bytes 6291460
  1.5 15.5 %all-to-all-start = ((s32[32,1,64]{2,1,0:T(1,128)}), s32[32,1,64]{2,1,0:T(1,128)S(1)}, u32[]{:S(2)}, u32[]{:S(2)}) async-start(s32[32,1,64]{2,1,0:T(1,128)} %broadcast_in_dim.16), calls=%async_computation | async-start | bytes 32768 | tf_op jit(solution)/shard_map/all_to_all | solution.py:29
  27.4 6.0 %copy-start.2 = (s32[4,16]{1,0:T(4,128)S(1)}, s32[4,16]{1,0:T(4,128)}, u32[]{:S(2)}) copy-start(s32[4,16]{1,0:T(4,128)} %param.10) | copy-start | bytes 772
  27.4 105.2 %all-to-all-start.1 = ((bf16[32,4,2,128,128]{4,3,2,1,0:T(8,128)(2,1)}), bf16[32,4,2,128,128]{4,3,2,1,0:T(8,128)(2,1)}, u32[]{:S(2)}, u32[]{:S(2)}) async-start(bf16[32,4,2,128,128]{4,3,2,1,0:T(8,128)(2,1)} %bitcast.58), calls=%async_computation.1 | async-start | bytes 16777216 | tf_op jit(solution)/shard_map/all_to_all | solution.py:41
  34.4 9.0 %copy-start.5 = (s32[8,224]{1,0:T(8,128)S(1)}, s32[8,224]{1,0:T(8,128)}, u32[]{:S(2)}) copy-start(s32[8,224]{1,0:T(8,128)} %param.14) | copy-start | bytes 21508
  34.4 9.1 %copy-start.1 = (s32[2048]{0:T(1024)S(1)}, s32[2048]{0:T(1024)}, u32[]{:S(2)}) copy-start(s32[2048]{0:T(1024)} %param.13) | copy-start | bytes 24580
  146.5 11.9 %copy-start.4 = (f32[4,448]{1,0:T(4,128)S(1)}, f32[4,448]{1,0:T(4,128)}, u32[]{:S(2)}) copy-start(f32[4,448]{1,0:T(4,128)} %param.12) | copy-start | bytes 21508
  147.9 21.8 %copy-start.3 = (f32[3,8,224]{2,1,0:T(8,128)S(1)}, f32[3,8,224]{2,1,0:T(8,128)}, u32[]{:S(2)}) copy-start(f32[3,8,224]{2,1,0:T(8,128)} %param.15) | copy-start | bytes 64516
  150.2 19.5 %all-to-all-start.2 = ((f32[8,1,224]{2,1,0:T(1,128)}), f32[8,1,224]{2,1,0:T(1,128)S(1)}, u32[]{:S(2)}, u32[]{:S(2)}) async-start(f32[8,1,224]{2,1,0:T(1,128)} %reshape.416), calls=%async_computation.2 | async-start | bytes 16384 | tf_op jit(solution)/shard_map/all_to_all | solution.py:60

commit v2 on v1

v2 whole, which is shorter than its diff:
```python
import functools

import jax
import jax.numpy as jnp
from jax import lax
from jax.experimental import pallas as pl
from jax.experimental.pallas import tpu as pltpu
from jax.sharding import PartitionSpec as P

CAPACITY = 4
MIB = 1024 * 1024


def send_kernel(lists_ref, density_ref, out_ref, sem, *, boxes, slots, own, rows, span):
    me = lax.axis_index("pts")
    bas = lax.axis_index("bas")
    home = lax.div(me, lax.axis_size("pts") // lax.axis_size("bas"))
    block = density_ref.shape[-1]

    def one_index(q, total):
        count = jnp.int32(0)
        for x in range(boxes):
            columns = [lists_ref[q, 0, x * slots + bas * own + j] - bas * span for j in range(own)]
            for t in range(own):
                wanted = lists_ref[q, 0, x * slots + home * own + t]
                row = wanted - me * rows
                mine = jnp.logical_and(row >= 0, row < rows)
                mine = jnp.logical_and(mine, jnp.logical_and(q != me, count < CAPACITY))

                @pl.when(mine)
                def _(row=row, columns=columns, count=count):
                    for j in range(own):
                        pltpu.make_async_copy(
                            density_ref.at[row, columns[j]],
                            out_ref.at[q, count, :, pl.ds(j * block, block)],
                            sem,
                        ).start()

                count = count + mine.astype(jnp.int32)
        return total + count

    total = lax.fori_loop(0, lists_ref.shape[0], one_index, jnp.int32(0))

    def drain(_, carry):
        for j in range(own):
            pltpu.make_async_copy(
                density_ref.at[0, 0], out_ref.at[0, 0, :, pl.ds(j * block, block)], sem
            ).wait()
        return carry

    lax.fori_loop(0, total, drain, 0)


def spread_kernel(atom_row_ref, column_ref, place_ref, value_ref, *, per_device, knbr):
    devices = place_ref.shape[1]
    owner = lax.broadcasted_iota(jnp.int32, (devices, 1), 0).astype(jnp.float32)
    place_ref[0] = jnp.where(owner == atom_row_ref[0], 1.0, 0.0).astype(jnp.bfloat16)
    lane = lax.broadcasted_iota(jnp.int32, (1, 128), 1)
    term = lax.rem(lane, 3 * per_device)
    axis = lax.div(term, per_device)
    inside = jnp.where(lane < 6 * per_device, (term - axis * per_device), -1).astype(jnp.float32)
    points = column_ref.shape[1]
    for k in range(knbr):
        cols = [column_ref[0, :, 4 * k + c : 4 * k + c + 1] for c in range(4)]
        value = jnp.where(axis == 0, cols[0], jnp.where(axis == 1, cols[1], cols[2]))
        value_ref[0, k * points : (k + 1) * points, :] = jnp.where(inside == cols[3], value, 0.0)


def split_parts(value, first):
    upper = value.astype(jnp.bfloat16).astype(jnp.float32)
    return jnp.where(first, upper, value - upper).astype(jnp.bfloat16)


def main_kernel(
    screen_ref,
    chi_ref,
    dchi_ref,
    arrived_ref,
    density_ref,
    weight_ref,
    atom_ref,
    place_ref,
    value_ref,
    out_ref,
    chi_buf,
    dchi_buf,
    block_buf,
    place_buf,
    value_buf,
    taken,
    chi_sem,
    dchi_sem,
    block_sem,
    place_sem,
    value_sem,
    *,
    rows,
    span,
    per_device,
):
    boxes, slots = screen_ref.shape
    block = density_ref.shape[-1]
    own = dchi_ref.shape[-1] // block
    me = lax.axis_index("pts")
    bas = lax.axis_index("bas")
    n_pts = lax.axis_size("pts")
    home = lax.div(me, n_pts // lax.axis_size("bas"))

    def chi_copy(x):
        return pltpu.make_async_copy(chi_ref.at[x], chi_buf.at[x], chi_sem.at[x])

    def dchi_copy(x):
        return pltpu.make_async_copy(dchi_ref.at[:, x], dchi_buf.at[x], dchi_sem.at[x])

    def place_copy(x):
        return pltpu.make_async_copy(place_ref.at[x], place_buf.at[x], place_sem.at[x])

    def value_copy(x):
        return pltpu.make_async_copy(value_ref.at[x], value_buf.at[x], value_sem.at[x])

    def clear(i, carry):
        taken[i] = 0
        return carry

    lax.fori_loop(0, n_pts, clear, 0)

    def block_copies(x):
        def one_slot(s, carry):
            wanted = screen_ref[x, s]
            owner = lax.div(wanted, rows)
            target = pl.ds(pl.multiple_of(s * block, block), block)

            @pl.when(owner == me)
            def _():
                for j in range(own):
                    column = screen_ref[x, bas * own + j] - bas * span
                    pltpu.make_async_copy(
                        density_ref.at[wanted - owner * rows, column],
                        block_buf.at[x, target, pl.ds(j * block, block)],
                        block_sem.at[x],
                    ).start()

            @pl.when(owner != me)
            def _():
                at = jnp.minimum(taken[owner], CAPACITY - 1)
                taken[owner] = at + 1
                pltpu.make_async_copy(
                    arrived_ref.at[owner, at], block_buf.at[x, target, :], block_sem.at[x]
                ).start()

            return carry

        lax.fori_loop(0, slots, one_slot, 0)

    for x in range(boxes):
        chi_copy(x).start()
        block_copies(x)
        dchi_copy(x).start()
        place_copy(x).start()
        value_copy(x).start()

    devices = out_ref.shape[0]
    owner_iota = lax.broadcasted_iota(jnp.int32, (devices, 1), 0)
    line = lax.broadcasted_iota(jnp.int32, (128, 1), 0)
    line_term = lax.rem(line, 3 * per_device)
    line_axis = lax.div(line_term, per_device)
    line_inside = jnp.where(line < 6 * per_device, line_term - line_axis * per_device, -1)
    lane = lax.broadcasted_iota(jnp.int32, (1, 128), 1)
    first_lane = lane < 3 * per_device
    first_line = line < 3 * per_device
    points = chi_buf.shape[1]
    knbr = value_buf.shape[1] // points
    total = jnp.zeros((devices, 128), jnp.float32)
    for x in range(boxes):
        chi_copy(x).wait()
        pltpu.make_async_copy(block_buf.at[x], block_buf.at[x], block_sem.at[x]).wait()
        fock = jnp.dot(chi_buf[x], block_buf[x], preferred_element_type=jnp.float32)
        width = own * block
        own_chi = chi_buf[x, :, pl.ds(pl.multiple_of(bas * width, width), width)]
        energy = jnp.sum(own_chi.astype(jnp.float32) * fock, axis=1, keepdims=True)
        weighted = fock * (-2.0 * weight_ref[x])
        dchi_copy(x).wait()
        terms = [
            jnp.sum(dchi_buf[x, d].astype(jnp.float32) * weighted, axis=0, keepdims=True)
            for d in range(3)
        ]
        atoms = jnp.concatenate(
            [
                atom_ref[pl.ds(screen_ref[x, bas * own + j] - bas * span, 1), :]
                for j in range(own)
            ],
            axis=1,
        )
        owners = lax.div(atoms, per_device)
        inside = atoms - owners * per_device
        spread = jnp.where(line_axis == 0, terms[0], jnp.where(line_axis == 1, terms[1], terms[2]))
        spread = jnp.where(line_inside == inside, spread, 0.0)
        onehot = jnp.where(owner_iota == owners, 1.0, 0.0).astype(jnp.bfloat16)
        total += lax.dot_general(
            onehot,
            split_parts(spread, first_line),
            (((1,), (1,)), ((), ())),
            preferred_element_type=jnp.float32,
        )
        place_copy(x).wait()
        value_copy(x).wait()
        becke = [
            split_parts(value_buf[x, k * points : (k + 1) * points, :] * energy, first_lane)
            for k in range(knbr)
        ]
        total += jnp.dot(
            place_buf[x], jnp.concatenate(becke, axis=0), preferred_element_type=jnp.float32
        )
    out_ref[...] = total + pltpu.roll(total, 128 - 3 * per_device, 1)


def shards(chi, dchi, screen, density, weights, basis_atom, neighbors, weight_grad):
    boxes, points, _ = chi.shape
    rows, span, block, _ = density.shape
    n_pts = lax.axis_size("pts")
    n_bas = lax.axis_size("bas")
    devices = n_pts * n_bas
    slots = screen.shape[1]
    own = slots // n_bas
    knbr = neighbors.shape[0]
    per_device = 12
    any_space = pl.BlockSpec(memory_space=pl.ANY)
    smem = pl.BlockSpec(memory_space=pltpu.SMEM)
    vmem = pl.BlockSpec(memory_space=pltpu.VMEM)

    flat = jnp.broadcast_to(screen.reshape(1, 1, -1), (n_pts, 1, boxes * slots))
    lists = lax.all_to_all(flat, "pts", split_axis=0, concat_axis=0, tiled=True)
    outgoing = pl.pallas_call(
        functools.partial(send_kernel, boxes=boxes, slots=slots, own=own, rows=rows, span=span),
        out_shape=jax.ShapeDtypeStruct((n_pts, CAPACITY, block, own * block), density.dtype),
        in_specs=[smem, any_space],
        out_specs=any_space,
        scratch_shapes=[pltpu.SemaphoreType.DMA],
        compiler_params=pltpu.CompilerParams(vmem_limit_bytes=4 * MIB),
    )(lists, density)
    arrived = lax.all_to_all(outgoing, "pts", split_axis=0, concat_axis=0, tiled=True)

    owner = neighbors // per_device
    packed = jnp.concatenate(
        [
            weight_grad,
            (neighbors - owner * per_device).astype(jnp.float32)[None],
            owner.astype(jnp.float32)[None],
        ]
    )
    packed = lax.all_gather(packed, "bas", axis=0)
    packed = packed.reshape(boxes, n_bas // boxes, 5, knbr, -1)
    columns = packed[:, :, :4].transpose(0, 1, 4, 3, 2).reshape(boxes, points, 4 * knbr)
    atom_rows = packed[:, :, 4].transpose(0, 2, 1, 3).reshape(boxes, 1, knbr * points)
    place, value = pl.pallas_call(
        functools.partial(spread_kernel, per_device=per_device, knbr=knbr),
        grid=(boxes,),
        out_shape=(
            jax.ShapeDtypeStruct((boxes, devices, knbr * points), jnp.bfloat16),
            jax.ShapeDtypeStruct((boxes, knbr * points, 128), jnp.float32),
        ),
        in_specs=[
            pl.BlockSpec((1, 1, knbr * points), lambda x: (x, 0, 0)),
            pl.BlockSpec((1, points, 4 * knbr), lambda x: (x, 0, 0)),
        ],
        out_specs=(
            pl.BlockSpec((1, devices, knbr * points), lambda x: (x, 0, 0)),
            pl.BlockSpec((1, knbr * points, 128), lambda x: (x, 0, 0)),
        ),
        compiler_params=pltpu.CompilerParams(vmem_limit_bytes=24 * MIB),
        cost_estimate=pl.CostEstimate(flops=20_000_000, bytes_accessed=16_000_000, transcendentals=0),
    )(atom_rows, columns)

    parts = pl.pallas_call(
        functools.partial(main_kernel, rows=rows, span=span, per_device=per_device),
        out_shape=jax.ShapeDtypeStruct((devices, 128), jnp.float32),
        in_specs=[smem] + [any_space] * 4 + [vmem] * 2 + [any_space] * 2,
        out_specs=vmem,
        scratch_shapes=[
            pltpu.VMEM(chi.shape, chi.dtype),
            pltpu.VMEM((boxes, 3) + dchi.shape[2:], dchi.dtype),
            pltpu.VMEM((boxes, slots * block, own * block), density.dtype),
            pltpu.VMEM(place.shape, place.dtype),
            pltpu.VMEM(value.shape, value.dtype),
            pltpu.SMEM((n_pts,), jnp.int32),
            pltpu.SemaphoreType.DMA((boxes,)),
            pltpu.SemaphoreType.DMA((boxes,)),
            pltpu.SemaphoreType.DMA((boxes,)),
            pltpu.SemaphoreType.DMA((boxes,)),
            pltpu.SemaphoreType.DMA((boxes,)),
        ],
        compiler_params=pltpu.CompilerParams(vmem_limit_bytes=52 * MIB),
        cost_estimate=pl.CostEstimate(flops=2_000_000_000, bytes_accessed=30_000_000, transcendentals=0),
    )(screen, chi, dchi, arrived, density, weights[:, :, None], basis_atom.reshape(span, block), place, value)
    parts = parts[:, : 3 * per_device].reshape(devices, 1, 3 * per_device)
    parts = lax.all_to_all(parts, ("pts", "bas"), split_axis=0, concat_axis=0, tiled=True)
    return jnp.sum(parts, axis=(0, 1)).reshape(3, -1)


def solution(mesh):
    in_specs = (
        P("pts", None, None),
        P(None, "pts", None, "bas"),
        P("pts", None),
        P("pts", "bas", None, None),
        P("pts", None),
        P("bas"),
        P(None, ("pts", "bas")),
        P(None, None, ("pts", "bas")),
    )
    out_specs = P(None, ("pts", "bas"))
    return jax.shard_map(shards, mesh=mesh, in_specs=in_specs, out_specs=out_specs, check_vma=False)
```

time: 215 us -> 177 us (0.82)
  blocking collectives: 27.8 us -> 69.1 us
  local copies, waits for them, and re-layouts: 49.4 us -> 13.5 us
  Pallas kernels: 0 us -> 31.4 us
  other arithmetic: 26.8 us -> 0.31 us
  waiting for transfers between devices: 81.6 us -> 57.5 us
  starting transfers between devices: 22.2 us -> 5.12 us
  matrix products: 6.54 us -> 0 us
    pallas_call x0 -> x3, Pallas kernels: none -> 31.4 us  [the longest x1 15.4 us: shards(): pl.pallas_call(functools.partial(main_kernel, rows=rows, span=span, per_d...]
    all_gather x0 -> x1, blocking collectives: none -> 25 us  [shards(): packed = lax.all_gather(packed, 'bas', axis=0)]
    gather x4 -> x0, local copies, waits for them, and re-layouts: 23 us -> none  [the longest x1 9.77 us: shards(): outgoing = density[send_row[..., None], send_columns]]
    scatter-add x2 -> x0, other arithmetic: 21 us -> none  [the longest x1 13.1 us: shards(): gradient = gradient.at[:, neighbors.reshape(-1)].add(becke_terms)]
    all_to_all x1, waiting for transfers between devices: 75.6 us -> 57.5 us  [shards(): lax.all_to_all(outgoing, 'pts', split_axis=0, concat_axis=0, tiled=True)]
    all_to_all x2 -> x0, starting transfers between devices: 16.8 us -> none  [the longest x1 8.59 us: shards(): lists = lax.all_to_all(flat, 'pts', split_axis=0, concat_axis=0, tiled=True)]
    all_to_all x0 -> x1, blocking collectives: none -> 15.3 us  [shards(): lists = lax.all_to_all(flat, 'pts', split_axis=0, concat_axis=0, tiled=True)]
    reshape x10 -> x3, local copies, waits for them, and re-layouts: 9.23 us -> 0.7 us  [the longest x2 0.53 us: shards(): packed[:, :, :4].transpose(0, 1, 4, 3, 2).reshape(boxes, points, 4 * knbr)]
  transfers between devices with their start and end apart: 3 -> 1, of which waited for: 2 -> 1; matrix products, arithmetic and copies ran while one was open for 17% -> 1% of each run, Pallas kernels for 0% -> 6%
where the time goes in v2:
time: 177 us
  blocking collectives  69.1 us (39%)
  waiting for transfers between devices  57.5 us (32%)
  Pallas kernels  31.4 us (18%)
  local copies, waits for them, and re-layouts  13.5 us (8%)
  starting transfers between devices  5.12 us (3%)
    all_to_all x1, waiting for transfers between devices, shards(): lax.all_to_all(outgoing, 'pts', split_axis=0, concat_axis=0, tiled=True)  57.5 us
    all_to_all x1, blocking collectives, shards(): lax.all_to_all(parts, ('pts', 'bas'), split_axis=0, concat_axis=0, tiled=...  28.8 us
    all_gather x1, blocking collectives, shards(): packed = lax.all_gather(packed, 'bas', axis=0)  25 us
    pallas_call x1, Pallas kernels, shards(): pl.pallas_call(functools.partial(main_kernel, rows=rows, span=span, per_d...  15.4 us
    all_to_all x1, blocking collectives, shards(): lists = lax.all_to_all(flat, 'pts', split_axis=0, concat_axis=0, tiled=True)  15.3 us
    unnamed x20, local copies, waits for them, and re-layouts  11 us
    pallas_call x1, Pallas kernels, shards(): pl.pallas_call(functools.partial(spread_kernel, per_device=per_device, kn...  9.89 us
    pallas_call x1, Pallas kernels, shards(): pl.pallas_call(functools.partial(send_kernel, boxes=boxes, slots=slots, o...  6.16 us
  transfers between devices with their start and end apart: 1, of which 1 were waited for; matrix products, arithmetic and copies ran while one was open for 1% of the time, Pallas kernels for 6%

profile of v2, /device:TPU:1, one launch (start us, length us, event | category | flops | bytes accessed | tf_op | source)
XLA Modules:
  0.0 177.2 jit_solution(6115966263774254597)
XLA Ops:
  0.0 0.8 broadcast_in_dim.16
  0.8 15.3 %all_to_all.15.lists_ref = s32[32,1,64]{2,1,0:T(1,128)S(1)} all-to-all(s32[32,1,64]{2,1,0:T(1,128)S(1)} %broadcast_in_dim.17), channel_id=1, replica_groups=mesh['pts'=32,'bas'=8] {'pts'}, dimensions={0} | all-to-all | bytes 16384 | tf_op jit(solution)/shard_map/all_to_all | solution.py:232
  16.1 0.0 copy-start.1
  16.1 1.6 copy-done.1
  17.7 6.2 %shard_map.82 = bf16[32,4,128,256]{3,2,1,0:T(8,128)(2,1)S(1)} custom-call(s32[32,1,64]{2,1,0:T(1,128)S(1)} %all_to_all.15.lists_ref, bf16[4,16,128,128]{3,2,1,0:T(8,128)(2,1)S(1)} %copy-done.1), custom_call_target="tpu_custom_call" | custom-call | tf_op jit(solution)/shard_map/pallas_call | solution.py:233
  23.9 0.0 copy-start
  23.9 3.2 %copy-done = bf16[32,4,128,256]{3,2,1,0:T(8,128)(2,1)} copy-done((bf16[32,4,128,256]{3,2,1,0:T(8,128)(2,1)}, bf16[32,4,128,256]{3,2,1,0:T(8,128)(2,1)S(1)}, u32[]{:S(2)}) %copy-start) | copy-done | bytes 8388632
  27.1 0.0 copy-start.8
  27.1 0.0 copy-start.6
  27.1 0.0 copy-start.7
  27.1 0.0 copy-start.5
  27.1 5.1 %all-to-all-start.1 = ((bf16[32,4,128,256]{3,2,1,0:T(8,128)(2,1)}), bf16[32,4,128,256]{3,2,1,0:T(8,128)(2,1)}, u32[]{:S(2)}, u32[]{:S(2)}) async-start(bf16[32,4,128,256]{3,2,1,0:T(8,128)(2,1)} %copy-done), calls=%async_computation.1 | async-start | bytes 16777216 | tf_op jit(solution)/shard_map/all_to_all | solution.py:241
  32.3 0.0 copy-done.8
  32.3 0.0 copy-done.6
  32.3 25.0 %all-gather = f32[40,8,224]{2,1,0:T(8,128)S(1)} all-gather(f32[5,8,224]{2,1,0:T(8,128)S(1)} %pad_maximum_fusion), channel_id=2, replica_groups=mesh['pts'=32,'bas'=8] {'bas'}, dimensions={0}, use_global_device_ids=true | all-gather | bytes 322560 | tf_op jit(solution)/shard_map/all_gather | solution.py:251
  57.4 0.2 copy.24
  57.6 0.2 reshape.25
  57.9 0.2 reshape.24.atom_row_ref
  58.0 0.3 copy.17.column_ref
  58.3 0.0 copy-done.7
  58.3 0.3 copy.18.weight_ref
  58.7 9.9 %shard_map.83 = (bf16[4,256,3584]{2,1,0:T(8,128)(2,1)S(1)}, f32[4,3584,128]{2,1,0:T(8,128)S(1)}) custom-call(f32[4,1,3584]{2,1,0:T(1,128)S(1)} %reshape.24.atom_row_ref, f32[4,448,32]{2,1,0:T(8,128)S(1)} %copy.17.column_ref), custom_call_target="tpu_custom_call" | custom-call | flops 20000000 | bytes 16000000 | tf_op jit(solution)/shard_map/pallas_call | solution.py:255
  68.6 0.0 copy-start.2
  68.6 2.9 %copy-done.2 = bf16[4,256,3584]{2,1,0:T(8,128)(2,1)} copy-done((bf16[4,256,3584]{2,1,0:T(8,128)(2,1)}, bf16[4,256,3584]{2,1,0:T(8,128)(2,1)S(1)}, u32[]{:S(2)}) %copy-start.2) | copy-done | bytes 7340056
  71.5 3.0 %copy-done.3 = f32[4,3584,128]{2,1,0:T(8,128)} copy-done((f32[4,3584,128]{2,1,0:T(8,128)}, f32[4,3584,128]{2,1,0:T(8,128)S(1)}, u32[]{:S(2)}) %copy-start.3) | copy-done | bytes 7340056
  74.5 57.5 %all-to-all-done.1.arrived_ref = bf16[32,4,128,256]{3,2,1,0:T(8,128)(2,1)} async-done(((bf16[32,4,128,256]{3,2,1,0:T(8,128)(2,1)}), bf16[32,4,128,256]{3,2,1,0:T(8,128)(2,1)}, u32[]{:S(2)}, u32[]{:S(2)}) %all-to-all-start.1) | async-done | bytes 8388640 | tf_op jit(solution)/shard_map/all_to_all | solution.py:241
  132.0 0.0 copy-done.4
  132.0 0.0 copy-done.5
  132.0 15.4 %shard_map.84 = f32[256,128]{1,0:T(8,128)S(1)} custom-call(s32[4,16]{1,0:T(4,128)S(1)} %copy-done.5, bf16[4,448,2048]{2,1,0:T(8,128)(2,1)} %chi_ref.1, bf16[3,4,448,256]{3,2,1,0:T(8,128)(2,1)} %dchi_ref.1, bf16[32,4,128,256]{3,2,1,0:T(8,128)(2,1)} %all-to-all-done.1.arrived_ref, bf16[4,16,128,128]{3,2,1,0:T(8,128)(2,1)} %density_ref.3, ...), custom_call_target="tpu_custom_call" | custom-call | flops 2000000000 | bytes 30000000 | tf_op jit(solution)/shard_map/pallas_call | solution.py:274
  147.4 28.8 %all_to_all.16 = f32[256,1,36]{2,1,0:T(1,128)S(1)} all-to-all(f32[256,1,36]{2,1,0:T(1,128)S(1)} %bitcast.21), channel_id=1, replica_groups=mesh['pts'=32,'bas'=8] {'pts','bas'}, dimensions={0} | all-to-all | bytes 73728 | tf_op jit(solution)/shard_map/all_to_all | solution.py:296
  176.2 0.3 reduce_sum.9
  176.5 0.7 reshape.27
  (8 shorter events, 0.1 us)
Async XLA Ops:
  16.1 1.6 copy-start.1
  23.9 3.2 %copy-start = (bf16[32,4,128,256]{3,2,1,0:T(8,128)(2,1)}, bf16[32,4,128,256]{3,2,1,0:T(8,128)(2,1)S(1)}, u32[]{:S(2)}) copy-start(bf16[32,4,128,256]{3,2,1,0:T(8,128)(2,1)S(1)} %shard_map.82) | copy-start | bytes 25165828
  27.1 5.2 %copy-start.8 = (s32[8,224]{1,0:T(8,128)S(1)}, s32[8,224]{1,0:T(8,128)}, u32[]{:S(2)}) copy-start(s32[8,224]{1,0:T(8,128)} %param.14) | copy-start | bytes 21508
  27.1 5.2 %copy-start.6 = (f32[3,8,224]{2,1,0:T(8,128)S(1)}, f32[3,8,224]{2,1,0:T(8,128)}, u32[]{:S(2)}) copy-start(f32[3,8,224]{2,1,0:T(8,128)} %param.15) | copy-start | bytes 64516
  27.1 31.2 %copy-start.7 = (f32[4,448]{1,0:T(4,128)S(1)}, f32[4,448]{1,0:T(4,128)}, u32[]{:S(2)}) copy-start(f32[4,448]{1,0:T(4,128)} %param.12) | copy-start | bytes 21508
  27.1 104.9 %copy-start.4 = (s32[2048]{0:T(1024)S(1)}, s32[2048]{0:T(1024)}, u32[]{:S(2)}) copy-start(s32[2048]{0:T(1024)} %param.13) | copy-start | bytes 24580
  27.1 104.9 %copy-start.5 = (s32[4,16]{1,0:T(4,128)S(1)}, s32[4,16]{1,0:T(4,128)}, u32[]{:S(2)}) copy-start(s32[4,16]{1,0:T(4,128)} %screen_ref.1) | copy-start | bytes 772
  27.1 104.9 %all-to-all-start.1 = ((bf16[32,4,128,256]{3,2,1,0:T(8,128)(2,1)}), bf16[32,4,128,256]{3,2,1,0:T(8,128)(2,1)}, u32[]{:S(2)}, u32[]{:S(2)}) async-start(bf16[32,4,128,256]{3,2,1,0:T(8,128)(2,1)} %copy-done), calls=%async_computation.1 | async-start | bytes 16777216 | tf_op jit(solution)/shard_map/all_to_all | solution.py:241
  68.6 2.9 %copy-start.2 = (bf16[4,256,3584]{2,1,0:T(8,128)(2,1)}, bf16[4,256,3584]{2,1,0:T(8,128)(2,1)S(1)}, u32[]{:S(2)}) copy-start(bf16[4,256,3584]{2,1,0:T(8,128)(2,1)S(1)} %get-tuple-element.7.place_ref) | copy-start | bytes 22020100
  71.5 3.0 %copy-start.3 = (f32[4,3584,128]{2,1,0:T(8,128)}, f32[4,3584,128]{2,1,0:T(8,128)S(1)}, u32[]{:S(2)}) copy-start(f32[4,3584,128]{2,1,0:T(8,128)S(1)} %get-tuple-element.8.value_ref) | copy-start | bytes 22020100

commit v3 on v1

v3 whole, which is shorter than its diff:
```python
import functools

import jax
import jax.numpy as jnp
from jax import lax
from jax.experimental import pallas as pl
from jax.experimental.pallas import tpu as pltpu
from jax.sharding import PartitionSpec as P

CAPACITY = 4
PACKED_ROWS = 2048
MIB = 1024 * 1024


def request_kernel(screen_hbm, table_ref, plan_ref, screen_ref, taken, sem, *, rows, span):
    load = pltpu.make_async_copy(screen_hbm, screen_ref, sem)
    load.start()
    boxes, slots = screen_ref.shape
    n_pts = table_ref.shape[0]
    me = lax.axis_index("pts")
    bas = lax.axis_index("bas")
    n_bas = lax.axis_size("bas")
    own = slots // n_bas
    home = lax.div(me, n_pts // n_bas)
    for i in range(n_pts):
        taken[i] = 0
        for c in range(CAPACITY):
            table_ref[i, 0, c] = 0
    load.wait()
    for x in range(boxes):
        columns = jnp.int32(0)
        for j in range(own):
            column = screen_ref[x, bas * own + j] - bas * span
            plan_ref[boxes * slots + x * 2 * own + j] = column
            plan_ref[boxes * slots + x * 2 * own + own + j] = screen_ref[x, home * own + j] - me * rows
            columns = columns * span + column
        for s in range(slots):
            wanted = screen_ref[x, s]
            owner = lax.shift_right_logical(wanted, rows.bit_length() - 1)
            at = taken[owner]
            taken[owner] = at + 1
            at = jnp.minimum(at, CAPACITY - 1)
            code = (wanted - owner * rows) * span**own + columns + 1
            table_ref[owner, 0, at] = jnp.where(owner == me, 0, code)
            plan_ref[x * slots + s] = owner * CAPACITY + at


def send_kernel(table_ref, density_ref, out_ref, sem, *, own):
    rows, span, block, _ = density_ref.shape

    def one_index(q, total):
        for c in range(CAPACITY):
            code = table_ref[q, 0, c]
            wanted = code > 0

            @pl.when(wanted)
            def _(code=code, c=c):
                rest = code - 1
                bits = span.bit_length() - 1
                row = jnp.bitwise_and(lax.shift_right_logical(rest, own * bits), rows - 1)
                for j in range(own):
                    shift = (own - 1 - j) * bits
                    column = jnp.bitwise_and(lax.shift_right_logical(rest, shift), span - 1)
                    pltpu.make_async_copy(
                        density_ref.at[row, column],
                        out_ref.at[q, c, :, pl.ds(j * block, block)],
                        sem,
                    ).start()

            total = total + wanted.astype(jnp.int32)
        return total

    total = lax.fori_loop(0, table_ref.shape[0], one_index, jnp.int32(0))

    def drain(_, carry):
        for j in range(own):
            pltpu.make_async_copy(
                density_ref.at[0, 0], out_ref.at[0, 0, :, pl.ds(j * block, block)], sem
            ).wait()
        return carry

    lax.fori_loop(0, total, drain, 0)


def pack_kernel(
    grad_ref,
    neighbor_ref,
    weight_ref,
    density_ref,
    packed_ref,
    weight_out_ref,
    density_out_ref,
    grad,
    neighbor,
    weight,
    turn,
    wide,
    tall,
    packed,
    sems,
    *,
    per_device,
):
    copies = [
        pltpu.make_async_copy(source, target, sems.at[i])
        for i, (source, target) in enumerate(
            [
                (grad_ref, grad),
                (neighbor_ref, neighbor),
                (weight_ref, weight),
                (density_ref, density_out_ref),
            ]
        )
    ]
    for copy in copies:
        copy.start()
    turn[...] = jnp.full_like(turn, -1.0)
    wide[...] = jnp.full_like(wide, -1.0)
    tall[...] = jnp.zeros_like(tall)
    for copy in copies[:3]:
        copy.wait()
    knbr, points = neighbor.shape
    owner = lax.div(neighbor[...], per_device)
    place = neighbor[...] - owner * per_device
    for d in range(3):
        wide[d, :, :points] = grad[d]
    wide[3, :, :points] = place.astype(jnp.float32)
    for c in range(4):
        for h in range(2):
            at = (c * 2 + h) * knbr
            packed[at : at + knbr, :] = wide[c, :, h * 128 : (h + 1) * 128]
    turn[:knbr, :points] = owner.astype(jnp.float32)
    packed[8 * knbr : 8 * knbr + 256, :] = turn[...].T
    packed_copy = pltpu.make_async_copy(packed, packed_ref.at[pl.ds(0, packed.shape[0])], sems.at[len(copies)])
    packed_copy.start()
    boxes, box_points = weight.shape
    tall[:boxes, :box_points] = weight[...]
    weight_out_ref[...] = tall[...].T[:box_points, :]
    for copy in copies[3:]:
        copy.wait()
    packed_copy.wait()


def in_hbm(array):
    return pltpu.with_memory_space_constraint(array, pltpu.HBM)


def spread_rows(values, places):
    inside = lax.broadcasted_iota(jnp.int32, (16, 1), 0).astype(jnp.float32) == places
    uppers, rests = [], []
    for value in values:
        upper = value.astype(jnp.bfloat16).astype(jnp.float32)
        uppers.append(jnp.where(inside, upper, 0.0))
        rests.append(jnp.where(inside, value - upper, 0.0))
    return jnp.concatenate(uppers + rests, axis=0).astype(jnp.bfloat16)


def owner_rows(owners, devices):
    line = lax.broadcasted_iota(jnp.int32, (devices, 1), 0).astype(jnp.float32).astype(jnp.bfloat16)
    one = jnp.ones((), jnp.bfloat16)
    zero = jnp.zeros((), jnp.bfloat16)
    return jnp.where(line == owners.astype(jnp.bfloat16), one, zero)


def along_lanes(left, right):
    return lax.dot_general(left, right, (((1,), (1,)), ((), ())), preferred_element_type=jnp.float32)


def main_kernel(
    plan_ref,
    chi_ref,
    dchi_ref,
    arrived_ref,
    density_ref,
    weight_ref,
    atom_ref,
    packed_ref,
    out_ref,
    chi_buf,
    block_buf,
    packed_buf,
    turn,
    chi_sem,
    block_sem,
    packed_sem,
    *,
    per_device,
    knbr,
):
    boxes = chi_buf.shape[0]
    block = density_ref.shape[-1]
    own = dchi_ref.shape[-1] // block
    slots = block_buf.shape[1] // block
    me = lax.axis_index("pts")
    bas = lax.axis_index("bas")
    n_bas = lax.axis_size("bas")
    halves = n_bas // boxes
    box_points = chi_buf.shape[1]
    points = box_points // halves
    devices = out_ref.shape[0]

    packed_copy = pltpu.make_async_copy(
        packed_ref.at[:, pl.ds(0, packed_buf.shape[1])], packed_buf, packed_sem
    )

    home = lax.div(me, lax.axis_size("pts") // n_bas)
    columns = [[plan_ref[boxes * slots + x * 2 * own + j] for j in range(own)] for x in range(boxes)]

    def block_copies(x):
        for i in range(slots):
            slot = lax.rem(home * own + i, slots)
            target = pl.ds(pl.multiple_of(slot * block, block), block)
            if i < own:
                row = plan_ref[boxes * slots + x * 2 * own + own + i]
                for j in range(own):
                    pltpu.make_async_copy(
                        density_ref.at[row, columns[x][j]],
                        block_buf.at[x, target, pl.ds(j * block, block)],
                        block_sem.at[x],
                    ).start()
            else:
                pltpu.make_async_copy(
                    arrived_ref.at[plan_ref[x * slots + slot]],
                    block_buf.at[x, target, :],
                    block_sem.at[x],
                ).start()

    def chi_copy(x):
        return pltpu.make_async_copy(chi_ref.at[x], chi_buf.at[x], chi_sem.at[x])

    for x in range(2):
        chi_copy(x).start()
        block_copies(x)
    packed_copy.start()

    owner_lane = lax.broadcasted_iota(jnp.int32, (1, devices), 1).astype(jnp.float32).astype(jnp.bfloat16)
    one = jnp.ones((), jnp.bfloat16)
    zero = jnp.zeros((), jnp.bfloat16)
    total = jnp.zeros((96, devices), jnp.float32)
    width = own * block
    for x in range(boxes):
        chi_copy(x).wait()
        pltpu.make_async_copy(block_buf.at[x], block_buf.at[x], block_sem.at[x]).wait()
        fock = jnp.dot(chi_buf[x], block_buf[x], preferred_element_type=jnp.float32)
        if x + 2 < boxes:
            chi_copy(x + 2).start()
            block_copies(x + 2)
        own_chi = chi_buf[x, :, pl.ds(pl.multiple_of(bas * width, width), width)]
        energy = jnp.sum(own_chi.astype(jnp.float32) * fock, axis=1, keepdims=True)
        weighted = fock * (-2.0 * weight_ref[:, x : x + 1])
        terms = [
            jnp.sum(dchi_ref[d, x].astype(jnp.float32) * weighted, axis=0, keepdims=True)
            for d in range(3)
        ]
        atoms = jnp.concatenate(
            [
                atom_ref[pl.ds(columns[x][j], 1), :]
                for j in range(own)
            ],
            axis=1,
        )
        owners = lax.div(atoms, per_device)
        inside = (atoms - owners * per_device).astype(jnp.float32)
        total += along_lanes(
            spread_rows(terms, inside), owner_rows(owners.astype(jnp.float32), devices)
        )
        if x == 0:
            packed_copy.wait()
        for h in range(halves):
            at = x * halves + h
            turn[:points, :] = jnp.broadcast_to(energy[h * points : (h + 1) * points], (points, 128))
            energy_row = turn[...].T[0:1, :]
            energy_row = jnp.where(
                lax.broadcasted_iota(jnp.int32, energy_row.shape, 1) < points, energy_row, 0.0
            )

            def lanes(c, at=at):
                return jnp.concatenate(
                    [packed_buf[at, (c * 2 + p) * knbr : (c * 2 + p + 1) * knbr, :] for p in range(2)],
                    axis=1,
                )

            grads = [lanes(d) * energy_row for d in range(3)]
            places = lanes(3)
            owners = packed_buf[at, 8 * knbr : 8 * knbr + 256, :].astype(jnp.bfloat16)
            left = jnp.concatenate(
                [
                    spread_rows([g[k : k + 1] for g in grads], places[k : k + 1])
                    for k in range(knbr)
                ],
                axis=1,
            )
            right = jnp.concatenate(
                [
                    jnp.where(owner_lane == owners[:, k : k + 1], one, zero)
                    for k in range(knbr)
                ],
                axis=0,
            )
            total += jnp.dot(left, right, preferred_element_type=jnp.float32)
    both = total[:48] + total[48:]
    parts = [both[d * 16 : d * 16 + per_device] for d in range(3)]
    parts.append(jnp.zeros((128 - 3 * per_device, devices), jnp.float32))
    out_ref[...] = jnp.concatenate(parts, axis=0).T


def run_main(plan, chi, dchi, arrived, density, weight_lines, atoms, gathered, devices, per_device):
    boxes = chi.shape[0]
    block = density.shape[-1]
    own = dchi.shape[-1] // block
    slots = chi.shape[-1] // block
    n_bas = lax.axis_size("bas")
    knbr = 8
    hbm = pl.BlockSpec(memory_space=pltpu.HBM)
    smem = pl.BlockSpec(memory_space=pltpu.SMEM)
    vmem = pl.BlockSpec(memory_space=pltpu.VMEM)
    return pl.pallas_call(
        functools.partial(main_kernel, per_device=per_device, knbr=knbr),
        out_shape=jax.ShapeDtypeStruct((devices, 128), jnp.float32),
        in_specs=[smem] + [hbm, vmem] + [hbm] * 2 + [vmem] * 2 + [hbm],
        out_specs=vmem,
        scratch_shapes=[
            pltpu.VMEM(chi.shape, chi.dtype),
            pltpu.VMEM((boxes, slots * block, own * block), density.dtype),
            pltpu.VMEM((n_bas, 8 * knbr + 256, 128), jnp.float32),
            pltpu.VMEM((256, 128), jnp.float32),
            pltpu.SemaphoreType.DMA((boxes,)),
            pltpu.SemaphoreType.DMA((boxes,)),
            pltpu.SemaphoreType.DMA,
        ],
        compiler_params=pltpu.CompilerParams(vmem_limit_bytes=28 * MIB),
        cost_estimate=pl.CostEstimate(flops=2_000_000_000, bytes_accessed=30_000_000, transcendentals=0),
    )(
        plan,
        chi,
        dchi,
        arrived,
        density,
        weight_lines,
        atoms,
        gathered,
    )


def shards(chi, dchi, screen, density, weights, basis_atom, neighbors, weight_grad):
    boxes, points, _ = chi.shape
    rows, span, block, _ = density.shape
    n_pts = lax.axis_size("pts")
    n_bas = lax.axis_size("bas")
    devices = n_pts * n_bas
    slots = screen.shape[1]
    own = slots // n_bas
    knbr = neighbors.shape[0]
    per_device = 12
    hbm = pl.BlockSpec(memory_space=pltpu.HBM)
    smem = pl.BlockSpec(memory_space=pltpu.SMEM)
    vmem = pl.BlockSpec(memory_space=pltpu.VMEM)

    table, plan = pl.pallas_call(
        functools.partial(request_kernel, rows=rows, span=span),
        out_shape=(
            jax.ShapeDtypeStruct((n_pts, 1, CAPACITY), jnp.int32),
            jax.ShapeDtypeStruct((boxes * (slots + 2 * own),), jnp.int32),
        ),
        in_specs=[hbm],
        out_specs=(smem, smem),
        scratch_shapes=[
            pltpu.SMEM(screen.shape, jnp.int32),
            pltpu.SMEM((n_pts,), jnp.int32),
            pltpu.SemaphoreType.DMA,
        ],
        compiler_params=pltpu.CompilerParams(vmem_limit_bytes=4 * MIB),
    )(in_hbm(screen))
    asked = lax.all_to_all(table, "pts", split_axis=0, concat_axis=0, tiled=True)
    packed, weight_lines, loaded = pl.pallas_call(
        functools.partial(pack_kernel, per_device=per_device),
        out_shape=(
            pltpu.HBM((PACKED_ROWS, 128), jnp.float32),
            jax.ShapeDtypeStruct((points, 128), jnp.float32),
            pltpu.VMEM(density.shape, density.dtype),
        ),
        in_specs=[hbm] * 4,
        out_specs=(hbm, vmem, vmem),
        scratch_shapes=[
            pltpu.VMEM(weight_grad.shape, jnp.float32),
            pltpu.VMEM(neighbors.shape, jnp.int32),
            pltpu.VMEM(weights.shape, jnp.float32),
            pltpu.VMEM((128, 256), jnp.float32),
            pltpu.VMEM((4, knbr, 256), jnp.float32),
            pltpu.VMEM((128, 512), jnp.float32),
            pltpu.VMEM((8 * knbr + 256, 128), jnp.float32),
            pltpu.SemaphoreType.DMA((5,)),
        ],
        compiler_params=pltpu.CompilerParams(vmem_limit_bytes=16 * MIB),
        cost_estimate=pl.CostEstimate(flops=5_000_000, bytes_accessed=2_000_000, transcendentals=0),
    )(
        in_hbm(weight_grad),
        in_hbm(neighbors),
        in_hbm(weights),
        in_hbm(density),
    )
    asked, weight_lines, packed = lax.optimization_barrier((asked, weight_lines, packed))
    gathered = in_hbm(lax.all_gather(packed, "bas", axis=0))
    outgoing = pl.pallas_call(
        functools.partial(send_kernel, own=own),
        out_shape=pltpu.HBM((n_pts, CAPACITY, block, own * block), density.dtype),
        in_specs=[smem, vmem],
        out_specs=hbm,
        scratch_shapes=[pltpu.SemaphoreType.DMA],
        compiler_params=pltpu.CompilerParams(vmem_limit_bytes=4 * MIB),
    )(asked, loaded)
    arrived = lax.all_to_all(outgoing, "pts", split_axis=0, concat_axis=0, tiled=True)

    parts = run_main(
        plan,
        in_hbm(chi),
        dchi,
        in_hbm(arrived.reshape(n_pts * CAPACITY, block, own * block)),
        in_hbm(density),
        weight_lines,
        basis_atom.reshape(span, block),
        gathered,
        devices,
        per_device,
    )
    parts = parts[:, : 3 * per_device].reshape(devices, 1, 3 * per_device)
    parts = lax.all_to_all(parts, ("pts", "bas"), split_axis=0, concat_axis=0, tiled=True)
    return jnp.sum(parts, axis=(0, 1)).reshape(3, per_device)


def solution(mesh):
    in_specs = (
        P("pts", None, None),
        P(None, "pts", None, "bas"),
        P("pts", None),
        P("pts", "bas", None, None),
        P("pts", None),
        P("bas"),
        P(None, ("pts", "bas")),
        P(None, None, ("pts", "bas")),
    )
    out_specs = P(None, ("pts", "bas"))
    return jax.shard_map(shards, mesh=mesh, in_specs=in_specs, out_specs=out_specs, check_vma=False)
```

time: 215 us -> 173 us (0.80)
  blocking collectives: 27.8 us -> 128 us
  waiting for transfers between devices: 81.6 us -> 5.21 us
  local copies, waits for them, and re-layouts: 49.4 us -> 0.68 us
  other arithmetic: 26.8 us -> 0.29 us
  Pallas kernels: 0 us -> 16.8 us
  starting transfers between devices: 22.2 us -> 8.64 us
  between operations: 0.32 us -> 13.5 us
  matrix products: 6.54 us -> 0 us
    all_to_all x0 -> x1, blocking collectives: none -> 102 us  [shards(): lax.all_to_all(outgoing, 'pts', split_axis=0, concat_axis=0, tiled=True)]
    all_to_all x3 -> x1, waiting for transfers between devices: 81.6 us -> 5.19 us  [shards(): lax.all_to_all(table, 'pts', split_axis=0, concat_axis=0, tiled=True)]
    gather x4 -> x0, local copies, waits for them, and re-layouts: 23 us -> none  [the longest x1 9.77 us: shards(): outgoing = density[send_row[..., None], send_columns]]
    scatter-add x2 -> x0, other arithmetic: 21 us -> none  [the longest x1 13.1 us: shards(): gradient = gradient.at[:, neighbors.reshape(-1)].add(becke_terms)]
    pallas_call x0 -> x4, Pallas kernels: none -> 16.8 us  [the longest x1 10.3 us: run_main(): pl.pallas_call(functools.partial(main_kernel, per_device=per_device, knbr...]
    all_to_all x3 -> x1, starting transfers between devices: 22.2 us -> 8.6 us  [shards(): lax.all_to_all(table, 'pts', split_axis=0, concat_axis=0, tiled=True)]
    unnamed x15 -> x4, local copies, waits for them, and re-layouts: 9.67 us -> 0.01 us
    reshape x11 -> x1, local copies, waits for them, and re-layouts: 9.9 us -> 0.66 us  [shards(): return jnp.sum(parts, axis=(0, 1)).reshape(3, per_device)]
  transfers between devices with their start and end apart: 3 -> 2, of which waited for: 2 -> 1; matrix products, arithmetic and copies ran while one was open for 17% -> 0% of each run, Pallas kernels for 0% -> 3%
where the time goes in v3:
time: 173 us
  blocking collectives  128 us (74%)
  Pallas kernels  16.8 us (10%)
  between operations  13.5 us (8%)
  starting transfers between devices  8.64 us (5%)
  waiting for transfers between devices  5.21 us (3%)
    all_to_all x1, blocking collectives, shards(): lax.all_to_all(outgoing, 'pts', split_axis=0, concat_axis=0, tiled=True)  102 us
    all_to_all x1, blocking collectives, shards(): lax.all_to_all(parts, ('pts', 'bas'), split_axis=0, concat_axis=0, tiled=...  25.9 us
    pallas_call x1, Pallas kernels, run_main(): pl.pallas_call(functools.partial(main_kernel, per_device=per_device, knbr...  10.3 us
    all_to_all x1, starting transfers between devices, shards(): lax.all_to_all(table, 'pts', split_axis=0, concat_axis=0, tiled=True)  8.6 us
    all_to_all x1, waiting for transfers between devices, shards(): lax.all_to_all(table, 'pts', split_axis=0, concat_axis=0, tiled=True)  5.19 us
  transfers between devices with their start and end apart: 2, of which 1 were waited for; matrix products, arithmetic and copies ran while one was open for 0% of the time, Pallas kernels for 3%

profile of v3, /device:TPU:1, one launch (start us, length us, event | category | flops | bytes accessed | tf_op | source)
XLA Modules:
  0.0 172.6 jit_solution(5268905013804096676)
XLA Ops:
  6.5 2.0 %shard_map.82 = (s32[32,1,4]{2,1,0:T(1,128)}, s32[80]{0:T(128)S(1)}) custom-call(s32[4,16]{1,0:T(4,128)} %screen_hbm.1), custom_call_target="tpu_custom_call" | custom-call | tf_op jit(solution)/shard_map/pallas_call | solution.py:359
  8.5 8.6 %all-to-all-start = ((s32[32,1,4]{2,1,0:T(1,128)}), s32[32,1,4]{2,1,0:T(1,128)S(1)}, u32[]{:S(2)}, u32[]{:S(2)}) async-start(s32[32,1,4]{2,1,0:T(1,128)} %get-tuple-element.14), calls=%async_computation | async-start | bytes 32768 | tf_op jit(solution)/shard_map/all_to_all | solution.py:374
  17.1 0.0 all-gather.3.cloned.1.call-start
  17.2 1.7 shard_map.83
  18.9 5.2 %all-to-all-done.table_ref = s32[32,1,4]{2,1,0:T(1,128)S(1)} async-done(((s32[32,1,4]{2,1,0:T(1,128)}), s32[32,1,4]{2,1,0:T(1,128)S(1)}, u32[]{:S(2)}, u32[]{:S(2)}) %all-to-all-start) | async-done | bytes 544 | tf_op jit(solution)/shard_map/all_to_all | solution.py:374
  24.1 0.0 all-gather.3.cloned.1.call-update
  24.1 2.8 %shard_map.84 = bf16[32,4,128,256]{3,2,1,0:T(8,128)(2,1)} custom-call(s32[32,1,4]{2,1,0:T(1,128)S(1)} %all-to-all-done.table_ref, bf16[4,16,128,128]{3,2,1,0:T(8,128)(2,1)S(1)} %get-tuple-element.18.density_ref), custom_call_target="tpu_custom_call" | custom-call | tf_op jit(solution)/shard_map/pallas_call | solution.py:404
  26.9 0.0 copy-start
  26.9 0.0 copy-start.1
  26.9 101.7 %all_to_all.15 = bf16[32,4,128,256]{3,2,1,0:T(8,128)(2,1)} all-to-all(bf16[32,4,128,256]{3,2,1,0:T(8,128)(2,1)} %shard_map.84), channel_id=1, replica_groups=mesh['pts'=32,'bas'=8] {'pts'}, dimensions={0} | all-to-all | bytes 16777216 | tf_op jit(solution)/shard_map/all_to_all | solution.py:412
  128.6 0.0 all-gather.3.cloned.1.call-done
  128.7 0.0 copy-done
  128.7 0.0 copy-done.1
  128.7 10.3 %shard_map.85 = f32[256,128]{1,0:T(8,128)S(1)} custom-call(s32[80]{0:T(128)S(1)} %get-tuple-element.13.plan_ref, bf16[4,448,2048]{2,1,0:T(8,128)(2,1)} %chi_ref.1, bf16[3,4,448,256]{3,2,1,0:T(8,128)(2,1)S(1)} %copy-done, bf16[128,128,256]{2,1,0:T(8,128)(2,1)} %bitcast.9, bf16[4,16,128,128]{3,2,1,0:T(8,128)(2,1)} %density_ref.3, ...), custom_call_target="tpu_custom_call" | custom-call | flops 2000000000 | bytes 30000000 | tf_op jit(solution)/shard_map/pallas_call | solution.py:317
  139.0 25.9 %all_to_all.16 = f32[256,1,36]{2,1,0:T(1,128)S(1)} all-to-all(f32[256,1,36]{2,1,0:T(1,128)S(1)} %bitcast.7), channel_id=1, replica_groups=mesh['pts'=32,'bas'=8] {'pts','bas'}, dimensions={0} | all-to-all | bytes 73728 | tf_op jit(solution)/shard_map/all_to_all | solution.py:427
  164.8 0.3 reduce_sum.9
  165.1 0.7 reshape.15
Async XLA Ops:
  8.5 15.5 %all-to-all-start = ((s32[32,1,4]{2,1,0:T(1,128)}), s32[32,1,4]{2,1,0:T(1,128)S(1)}, u32[]{:S(2)}, u32[]{:S(2)}) async-start(s32[32,1,4]{2,1,0:T(1,128)} %get-tuple-element.14), calls=%async_computation | async-start | bytes 32768 | tf_op jit(solution)/shard_map/all_to_all | solution.py:374
  17.1 111.5 %all-gather.3.cloned.1.call-start = ((), (), s32[]{:S(2)}) async-start(), calls=%async_computation.3 | async-start | bytes 9437184 | tf_op jit(solution)/shard_map/all_gather | solution.py:403
  26.9 101.8 %copy-start = (bf16[3,4,448,256]{3,2,1,0:T(8,128)(2,1)S(1)}, bf16[3,4,448,256]{3,2,1,0:T(8,128)(2,1)}, u32[]{:S(2)}) copy-start(bf16[3,4,448,256]{3,2,1,0:T(8,128)(2,1)} %dchi_ref.1) | copy-start | bytes 8257540
  26.9 101.8 %copy-start.1 = (s32[2048]{0:T(1024)S(1)}, s32[2048]{0:T(1024)}, u32[]{:S(2)}) copy-start(s32[2048]{0:T(1024)} %param.13) | copy-start | bytes 24580
Sparse Core Ops, SparseCore 0:
  24.2 93.2 all-gather.2

commit v4 on v3

v4 whole, which is shorter than its diff:
```python
import functools

import jax
import jax.numpy as jnp
from jax import lax
from jax.experimental import pallas as pl
from jax.experimental.pallas import tpu as pltpu
from jax.sharding import PartitionSpec as P

PACKED_ROWS = 1024
MIB = 1024 * 1024


def first_kernel(
    density_ref,
    screen_ref,
    grad_ref,
    neighbor_ref,
    weight_ref,
    *refs,
    group,
    per_device,
):
    outs = refs[:group]
    packed_ref, weight_out_ref, lists_ref = refs[group : group + 3]
    held, grad, neighbor, weight, screen, turn, wide, tall, packed, load_sem, sem, small_sem = refs[group + 3 :]
    part = density_ref.shape[2] // group
    place = lax.rem(lax.axis_index("pts"), group)
    rows = density_ref.shape[0]
    loads = [
        pltpu.make_async_copy(density_ref.at[i], held.at[i], load_sem.at[i]) for i in range(rows)
    ]
    small = [
        pltpu.make_async_copy(source, target, small_sem.at[i])
        for i, (source, target) in enumerate(
            [(screen_ref, screen), (grad_ref, grad), (neighbor_ref, neighbor), (weight_ref, weight)]
        )
    ]
    for load in loads:
        load.start()
    for load in small:
        load.start()
    turn[...] = jnp.full_like(turn, -1.0)
    wide[...] = jnp.full_like(wide, -1.0)
    tall[...] = jnp.zeros_like(tall)
    copies = []
    for i in range(rows):
        loads[i].wait()
        for d in reversed(range(group)):
            start = pl.multiple_of(jnp.bitwise_xor(place, d) * part, part)
            copies.append(
                pltpu.make_async_copy(held.at[i, :, pl.ds(start, part)], outs[d].at[i], sem.at[d, i])
            )
            copies[-1].start()
    for load in small:
        load.wait()
    boxes, slots = screen.shape
    line = jnp.concatenate([screen[x : x + 1, :] for x in range(boxes)], axis=1)
    for q in range(lists_ref.shape[0]):
        lists_ref[q] = line
    knbr, points = neighbor.shape
    owner = lax.div(neighbor[...], per_device)
    inside = neighbor[...] - owner * per_device
    for d in range(3):
        wide[d, :, :points] = grad[d]
    wide[3, :, :points] = inside.astype(jnp.float32)
    for c in range(4):
        for h in range(2):
            at = (c * 2 + h) * knbr
            packed[at : at + knbr, :] = wide[c, :, h * 128 : (h + 1) * 128]
    turn[:knbr, :points] = owner.astype(jnp.float32)
    packed[8 * knbr : 8 * knbr + 256, :] = turn[...].T
    packed_copy = pltpu.make_async_copy(packed, packed_ref.at[pl.ds(0, packed.shape[0])], small_sem.at[4])
    packed_copy.start()
    boxes, box_points = weight.shape
    tall[:boxes, :box_points] = weight[...]
    weight_out_ref[...] = tall[...].T[:box_points, :]
    for copy in copies:
        copy.wait()
    packed_copy.wait()


def send_kernel(lists_ref, *refs, boxes, slots, own):
    *pieces, out_ref, held, stage, load_sem, sem = refs
    group = len(pieces)
    rows, span = pieces[0].shape[:2]
    block = held.shape[-1]
    me = lax.axis_index("pts")
    bas = lax.axis_index("bas")
    place = lax.rem(me, group)
    home = lax.div(me, group)
    loads = []
    for d, piece in enumerate(pieces):
        start = jnp.bitwise_xor(place, d) * rows
        loads.append(pltpu.make_async_copy(piece, held.at[pl.ds(start, rows)], load_sem.at[d]))
        loads[-1].start()
    for load in loads:
        load.wait()

    def one_index(q, carry):
        found = []
        for x in range(boxes):
            columns = [lists_ref[q, 0, x * slots + bas * own + j] - bas * span for j in range(own)]
            for t in range(own):
                row = lists_ref[q, 0, x * slots + home * own + t] - home * group * rows
                found.append([held[row, columns[j]] for j in range(own)])
        for i, parts in enumerate(found):
            stage[q, i] = jnp.concatenate(parts, axis=1)
        pltpu.make_async_copy(stage.at[q], out_ref.at[q], sem).start()
        return carry

    lax.fori_loop(0, lists_ref.shape[0], one_index, 0, unroll=2)
    pltpu.make_async_copy(stage, out_ref, sem).wait()


def in_hbm(array):
    return pltpu.with_memory_space_constraint(array, pltpu.HBM)


def spread_rows(values, places):
    inside = lax.broadcasted_iota(jnp.int32, (16, 1), 0).astype(jnp.float32) == places
    uppers, rests = [], []
    for value in values:
        upper = value.astype(jnp.bfloat16).astype(jnp.float32)
        uppers.append(jnp.where(inside, upper, 0.0))
        rests.append(jnp.where(inside, value - upper, 0.0))
    return jnp.concatenate(uppers + rests, axis=0).astype(jnp.bfloat16)


def owner_rows(owners, devices):
    line = lax.broadcasted_iota(jnp.int32, (devices, 1), 0).astype(jnp.float32).astype(jnp.bfloat16)
    one = jnp.ones((), jnp.bfloat16)
    zero = jnp.zeros((), jnp.bfloat16)
    return jnp.where(line == owners.astype(jnp.bfloat16), one, zero)


def along_lanes(left, right):
    return lax.dot_general(left, right, (((1,), (1,)), ((), ())), preferred_element_type=jnp.float32)


def main_kernel(
    screen_ref,
    chi_ref,
    dchi_ref,
    arrived_ref,
    weight_ref,
    atom_ref,
    packed_ref,
    out_ref,
    chi_buf,
    block_buf,
    packed_buf,
    turn,
    chi_sem,
    block_sem,
    packed_sem,
    *,
    per_device,
    knbr,
):
    boxes = chi_buf.shape[0]
    span, block = atom_ref.shape
    own = dchi_ref.shape[-1] // block
    bas = lax.axis_index("bas")
    n_bas = lax.axis_size("bas")
    halves = n_bas // boxes
    box_points = chi_buf.shape[1]
    points = box_points // halves
    devices = out_ref.shape[0]

    packed_copy = pltpu.make_async_copy(
        packed_ref.at[:, pl.ds(0, packed_buf.shape[1])], packed_buf, packed_sem
    )
    columns = [[screen_ref[x, bas * own + j] - bas * span for j in range(own)] for x in range(boxes)]

    def block_copies(x):
        for t in range(own):
            pltpu.make_async_copy(
                arrived_ref.at[:, :, x * own + t], block_buf.at[x, :, t], block_sem.at[x]
            ).start()

    def chi_copy(x):
        return pltpu.make_async_copy(chi_ref.at[x], chi_buf.at[x], chi_sem.at[x])

    for x in range(2):
        chi_copy(x).start()
        block_copies(x)
    packed_copy.start()

    owner_lane = lax.broadcasted_iota(jnp.int32, (1, devices), 1).astype(jnp.float32).astype(jnp.bfloat16)
    one = jnp.ones((), jnp.bfloat16)
    zero = jnp.zeros((), jnp.bfloat16)
    total = jnp.zeros((96, devices), jnp.float32)
    width = own * block
    for x in range(boxes):
        chi_copy(x).wait()
        pltpu.make_async_copy(block_buf.at[x], block_buf.at[x], block_sem.at[x]).wait()
        blocks = block_buf[x].reshape(chi_buf.shape[2], own * block)
        fock = jnp.dot(chi_buf[x], blocks, preferred_element_type=jnp.float32)
        if x + 2 < boxes:
            chi_copy(x + 2).start()
            block_copies(x + 2)
        own_chi = chi_buf[x, :, pl.ds(pl.multiple_of(bas * width, width), width)]
        energy = jnp.sum(own_chi.astype(jnp.float32) * fock, axis=1, keepdims=True)
        weighted = fock * (-2.0 * weight_ref[:, x : x + 1])
        terms = [
            jnp.sum(dchi_ref[d, x].astype(jnp.float32) * weighted, axis=0, keepdims=True)
            for d in range(3)
        ]
        atoms = jnp.concatenate(
            [
                atom_ref[pl.ds(columns[x][j], 1), :]
                for j in range(own)
            ],
            axis=1,
        )
        owners = lax.div(atoms, per_device)
        inside = (atoms - owners * per_device).astype(jnp.float32)
        total += along_lanes(
            spread_rows(terms, inside), owner_rows(owners.astype(jnp.float32), devices)
        )
        if x == 0:
            packed_copy.wait()
        for h in range(halves):
            at = x * halves + h
            turn[:points, :] = jnp.broadcast_to(energy[h * points : (h + 1) * points], (points, 128))
            energy_row = turn[...].T[0:1, :]
            energy_row = jnp.where(
                lax.broadcasted_iota(jnp.int32, energy_row.shape, 1) < points, energy_row, 0.0
            )

            def lanes(c, at=at):
                return jnp.concatenate(
                    [packed_buf[at, (c * 2 + p) * knbr : (c * 2 + p + 1) * knbr, :] for p in range(2)],
                    axis=1,
                )

            grads = [lanes(d) * energy_row for d in range(3)]
            places = lanes(3)
            owners = packed_buf[at, 8 * knbr : 8 * knbr + 256, :].astype(jnp.bfloat16)
            left = jnp.concatenate(
                [
                    spread_rows([g[k : k + 1] for g in grads], places[k : k + 1])
                    for k in range(knbr)
                ],
                axis=1,
            )
            right = jnp.concatenate(
                [
                    jnp.where(owner_lane == owners[:, k : k + 1], one, zero)
                    for k in range(knbr)
                ],
                axis=0,
            )
            total += jnp.dot(left, right, preferred_element_type=jnp.float32)
    both = total[:48] + total[48:]
    parts = [both[d * 16 : d * 16 + per_device] for d in range(3)]
    parts.append(jnp.zeros((128 - 3 * per_device, devices), jnp.float32))
    out_ref[...] = jnp.concatenate(parts, axis=0).T


def run_main(screen, chi, dchi, arrived, weight_lines, atoms, gathered, devices, per_device):
    boxes = chi.shape[0]
    n_bas = lax.axis_size("bas")
    knbr = 8
    hbm = pl.BlockSpec(memory_space=pltpu.HBM)
    smem = pl.BlockSpec(memory_space=pltpu.SMEM)
    vmem = pl.BlockSpec(memory_space=pltpu.VMEM)
    ranges, group, asked, part, width = arrived.shape
    return pl.pallas_call(
        functools.partial(main_kernel, per_device=per_device, knbr=knbr),
        out_shape=jax.ShapeDtypeStruct((devices, 128), jnp.float32),
        in_specs=[smem, hbm, vmem, hbm, vmem, vmem, hbm],
        out_specs=vmem,
        scratch_shapes=[
            pltpu.VMEM(chi.shape, chi.dtype),
            pltpu.VMEM((boxes, ranges, asked // boxes, group, part, width), arrived.dtype),
            pltpu.VMEM((n_bas, 8 * knbr + 256, 128), jnp.float32),
            pltpu.VMEM((256, 128), jnp.float32),
            pltpu.SemaphoreType.DMA((boxes,)),
            pltpu.SemaphoreType.DMA((boxes,)),
            pltpu.SemaphoreType.DMA,
        ],
        compiler_params=pltpu.CompilerParams(vmem_limit_bytes=28 * MIB),
        cost_estimate=pl.CostEstimate(flops=2_000_000_000, bytes_accessed=30_000_000, transcendentals=0),
    )(
        screen,
        chi,
        dchi,
        arrived,
        weight_lines,
        atoms,
        gathered,
    )


def shards(chi, dchi, screen, density, weights, basis_atom, neighbors, weight_grad):
    boxes, points, _ = chi.shape
    rows, span, block, _ = density.shape
    n_pts = lax.axis_size("pts")
    n_bas = lax.axis_size("bas")
    devices = n_pts * n_bas
    slots = screen.shape[1]
    own = slots // n_bas
    knbr = neighbors.shape[0]
    per_device = 12
    hbm = pl.BlockSpec(memory_space=pltpu.HBM)
    smem = pl.BlockSpec(memory_space=pltpu.SMEM)
    vmem = pl.BlockSpec(memory_space=pltpu.VMEM)

    group = n_pts // n_bas
    *pieces, packed, weight_lines, flat = pl.pallas_call(
        functools.partial(first_kernel, group=group, per_device=per_device),
        out_shape=[pltpu.HBM((rows, span, block // group, block), density.dtype)] * group
        + [
            pltpu.HBM((PACKED_ROWS, 128), jnp.float32),
            jax.ShapeDtypeStruct((points, 128), jnp.float32),
            jax.ShapeDtypeStruct((n_pts, 1, boxes * slots), jnp.int32),
        ],
        in_specs=[hbm] * 5,
        out_specs=[hbm] * (group + 1) + [vmem] * 2,
        scratch_shapes=[
            pltpu.VMEM(density.shape, density.dtype),
            pltpu.VMEM(weight_grad.shape, jnp.float32),
            pltpu.VMEM(neighbors.shape, jnp.int32),
            pltpu.VMEM(weights.shape, jnp.float32),
            pltpu.VMEM(screen.shape, jnp.int32),
            pltpu.VMEM((128, 256), jnp.float32),
            pltpu.VMEM((4, knbr, 256), jnp.float32),
            pltpu.VMEM((128, 512), jnp.float32),
            pltpu.VMEM((8 * knbr + 256, 128), jnp.float32),
            pltpu.SemaphoreType.DMA((rows,)),
            pltpu.SemaphoreType.DMA((group, rows)),
            pltpu.SemaphoreType.DMA((5,)),
        ],
        compiler_params=pltpu.CompilerParams(vmem_limit_bytes=12 * MIB),
    )(in_hbm(density), in_hbm(screen), in_hbm(weight_grad), in_hbm(neighbors), in_hbm(weights))
    pieces = [in_hbm(pieces[0])] + [
        lax.ppermute(pieces[d], "pts", [(p, p ^ d) for p in range(n_pts)]) for d in range(1, group)
    ]
    lists = lax.all_to_all(flat, "pts", split_axis=0, concat_axis=0, tiled=True)
    gathered = in_hbm(lax.all_gather(packed, "bas", axis=0))
    outgoing = pl.pallas_call(
        functools.partial(send_kernel, boxes=boxes, slots=slots, own=own),
        out_shape=pltpu.HBM((n_pts, boxes * own, block // group, own * block), density.dtype),
        in_specs=[smem] + [hbm] * group,
        out_specs=hbm,
        scratch_shapes=[
            pltpu.VMEM((group * rows, span, block // group, block), density.dtype),
            pltpu.VMEM((n_pts, boxes * own, block // group, own * block), density.dtype),
            pltpu.SemaphoreType.DMA((group,)),
            pltpu.SemaphoreType.DMA,
        ],
        compiler_params=pltpu.CompilerParams(vmem_limit_bytes=12 * MIB),
    )(lists, *pieces)
    arrived = lax.all_to_all(outgoing, "pts", split_axis=0, concat_axis=0, tiled=True)
    arrived = arrived.reshape(n_bas, group, boxes * own, block // group, own * block)

    parts = run_main(
        screen,
        in_hbm(chi),
        dchi,
        in_hbm(arrived),
        weight_lines,
        basis_atom.reshape(span, block),
        gathered,
        devices,
        per_device,
    )
    parts = parts[:, : 3 * per_device].reshape(devices, 1, 3 * per_device)
    parts = lax.all_to_all(parts, ("pts", "bas"), split_axis=0, concat_axis=0, tiled=True)
    return jnp.sum(parts, axis=(0, 1)).reshape(3, per_device)


def solution(mesh):
    in_specs = (
        P("pts", None, None),
        P(None, "pts", None, "bas"),
        P("pts", None),
        P("pts", "bas", None, None),
        P("pts", None),
        P("bas"),
        P(None, ("pts", "bas")),
        P(None, None, ("pts", "bas")),
    )
    out_specs = P(None, ("pts", "bas"))
    return jax.shard_map(shards, mesh=mesh, in_specs=in_specs, out_specs=out_specs, check_vma=False)
```

time: 173 us -> 144 us (0.83)
  blocking collectives: 128 us -> 107 us
  waiting for transfers between devices: 5.21 us -> 0.03 us
  starting transfers between devices: 8.64 us -> 5.06 us
    all_to_all x1, blocking collectives: 102 us -> 56.4 us  [shards(): lax.all_to_all(outgoing, 'pts', split_axis=0, concat_axis=0, tiled=True)]
    all_to_all x0 -> x1, blocking collectives: none -> 26.6 us  [shards(): lists = lax.all_to_all(flat, 'pts', split_axis=0, concat_axis=0, tiled=True)]
    all_to_all x1 -> x0, starting transfers between devices: 8.6 us -> none  [shards(): lax.all_to_all(table, 'pts', split_axis=0, concat_axis=0, tiled=True)]
    all_to_all x1 -> x0, waiting for transfers between devices: 5.19 us -> none  [shards(): lax.all_to_all(table, 'pts', split_axis=0, concat_axis=0, tiled=True)]
    ppermute x0 -> x3, starting transfers between devices: none -> 5.06 us  [shards(): lax.ppermute(pieces[d], 'pts', [(p, p ^ d) for p in range(n_pts)])]
    pallas_call x3 -> x2, Pallas kernels: 6.45 us -> 7.21 us  [the longest x1 4.56 us: shards(): pl.pallas_call(functools.partial(send_kernel, boxes=boxes, slots=slots, o...]
  transfers between devices with their start and end apart: 2 -> 4, of which waited for: 1 -> 0; matrix products, arithmetic and copies ran while one was open for 0% -> 0% of each run, Pallas kernels for 3% -> 3%
where the time goes in v4:
time: 144 us
  blocking collectives  107 us (74%)
  Pallas kernels  17.1 us (12%)
  between operations  13.4 us (9%)
  starting transfers between devices  5.06 us (4%)
    all_to_all x1, blocking collectives, shards(): lax.all_to_all(outgoing, 'pts', split_axis=0, concat_axis=0, tiled=True)  56.4 us
    all_to_all x1, blocking collectives, shards(): lists = lax.all_to_all(flat, 'pts', split_axis=0, concat_axis=0, tiled=True)  26.6 us
    all_to_all x1, blocking collectives, shards(): lax.all_to_all(parts, ('pts', 'bas'), split_axis=0, concat_axis=0, tiled=...  24.5 us
    pallas_call x1, Pallas kernels, run_main(): pl.pallas_call(functools.partial(main_kernel, per_device=per_device, knbr...  9.88 us
    ppermute x3, starting transfers between devices, shards(): lax.ppermute(pieces[d], 'pts', [(p, p ^ d) for p in range(n_pts)])  5.06 us
    pallas_call x1, Pallas kernels, shards(): pl.pallas_call(functools.partial(send_kernel, boxes=boxes, slots=slots, o...  4.56 us
  transfers between devices with their start and end apart: 4, of which 0 were waited for; matrix products, arithmetic and copies ran while one was open for 0% of the time, Pallas kernels for 3%

profile of v4, /device:TPU:1, one launch (start us, length us, event | category | flops | bytes accessed | tf_op | source)
XLA Modules:
  0.0 144.0 jit_solution(7051361341572649744)
XLA Ops:
  6.5 0.0 all-gather.3.cloned.1.call-start
  6.5 2.7 %shard_map.82 = (bf16[4,16,32,128]{3,2,1,0:T(8,128)(2,1)}, bf16[4,16,32,128]{3,2,1,0:T(8,128)(2,1)}, bf16[4,16,32,128]{3,2,1,0:T(8,128)(2,1)}, bf16[4,16,32,128]...) custom-call(bf16[4,16,128,128]{3,2,1,0:T(8,128)(2,1)} %density_ref.1, ...), custom_call_target="tpu_custom_call" | custom-call | tf_op jit(solution)/shard_map/pallas_call | solution.py:312
  9.2 0.0 all-gather.3.cloned.1.call-update
  9.2 3.3 %collective-permute-start = (bf16[4,16,32,128]{3,2,1,0:T(8,128)(2,1)}, bf16[4,16,32,128]{3,2,1,0:T(8,128)(2,1)S(1)}, u32[]{:S(2)}, u32[]{:S(2)}) collective-permute-start(bf16[4,16,32,128]{3,2,1,0:T(8,128)(2,1)} %get-tuple-element.14), channel_id=1, source_target_pairs={{0,8},{8,0},{16,24},{24,16},{32,40},{40,32},{48,56},{56,48},{64,72... | collective-permute-start | bytes 1572872 | tf_op jit(solution)/shard_map/ppermute | solution.py:339
  12.6 0.0 collective-permute-start.1
  12.6 1.7 %collective-permute-start.2 = (bf16[4,16,32,128]{3,2,1,0:T(8,128)(2,1)}, bf16[4,16,32,128]{3,2,1,0:T(8,128)(2,1)S(1)}, u32[]{:S(2)}, u32[]{:S(2)}) collective-permute-start(bf16[4,16,32,128]{3,2,1,0:T(8,128)(2,1)} %get-tuple-element.16), channel_id=1, source_target_pairs={{0,24},{8,16},{16,8},{24,0},{32,56},{40,48},{48,40},{56,32},{64,88... | collective-permute-start | bytes 1572872 | tf_op jit(solution)/shard_map/ppermute | solution.py:339
  14.3 26.6 %all_to_all.15.lists_ref = s32[32,1,64]{2,1,0:T(1,128)S(1)} all-to-all(s32[32,1,64]{2,1,0:T(1,128)S(1)} %get-tuple-element.12), channel_id=1, replica_groups=mesh['pts'=32,'bas'=8] {'pts'}, dimensions={0} | all-to-all | bytes 16384 | tf_op jit(solution)/shard_map/all_to_all | solution.py:341
  40.9 0.0 collective-permute-done.refs_1_
  40.9 0.0 collective-permute-done.1.refs_2_
  40.9 0.0 collective-permute-done.2.refs_3_
  40.9 4.6 %shard_map.83 = bf16[32,8,32,256]{3,2,1,0:T(8,128)(2,1)} custom-call(s32[32,1,64]{2,1,0:T(1,128)S(1)} %all_to_all.15.lists_ref, bf16[4,16,32,128]{3,2,1,0:T(8,128)(2,1)} %get-tuple-element.13.refs_0_, bf16[4,16,32,128]{3,2,1,0:T(8,128)(2,1)S(1)} %collective-permute-done.refs_1_, bf16[4,16,32,128]{3,2,1,0:T(8,128)(2,1)S(1)} %collective-permute-done.1.refs_2_, ...), custom_call_target="tpu_custom_call" | custom-call | tf_op jit(solution)/shard_map/pallas_call | solution.py:343
  45.5 0.0 copy-start
  45.5 0.0 copy-start.1
  45.5 0.0 copy-start.2
  45.5 56.4 %all_to_all.16 = bf16[32,8,32,256]{3,2,1,0:T(8,128)(2,1)} all-to-all(bf16[32,8,32,256]{3,2,1,0:T(8,128)(2,1)} %shard_map.83), channel_id=1, replica_groups=mesh['pts'=32,'bas'=8] {'pts'}, dimensions={0} | all-to-all | bytes 8388608 | tf_op jit(solution)/shard_map/all_to_all | solution.py:356
  101.9 0.0 all-gather.3.cloned.1.call-done
  101.9 0.0 copy-done
  101.9 0.0 copy-done.1
  101.9 0.0 copy-done.2
  101.9 9.9 %shard_map.84 = f32[256,128]{1,0:T(8,128)S(1)} custom-call(s32[4,16]{1,0:T(4,128)S(1)} %copy-done.2, bf16[4,448,2048]{2,1,0:T(8,128)(2,1)} %chi_ref.1, bf16[3,4,448,256]{3,2,1,0:T(8,128)(2,1)S(1)} %copy-done, bf16[8,4,8,32,256]{4,3,2,1,0:T(8,128)(2,1)} %bitcast.9, f32[448,128]{1,0:T(8,128)S(1)} %get-tuple-element.17.weight_ref, s32[16,128]{1,0:T(8,128)S(1)} %bitcast.8, ...), custom_call_target="tpu_custom_call" | custom-call | flops 2000000000 | bytes 30000000 | tf_op jit(solution)/shard_map/pallas_call | solution.py:270
  111.8 24.5 %all_to_all.17 = f32[256,1,36]{2,1,0:T(1,128)S(1)} all-to-all(f32[256,1,36]{2,1,0:T(1,128)S(1)} %bitcast.7), channel_id=1, replica_groups=mesh['pts'=32,'bas'=8] {'pts','bas'}, dimensions={0} | all-to-all | bytes 73728 | tf_op jit(solution)/shard_map/all_to_all | solution.py:371
  136.2 0.3 reduce_sum.9
  136.5 0.7 reshape.15
Async XLA Ops:
  6.5 95.4 %all-gather.3.cloned.1.call-start = ((), (), s32[]{:S(2)}) async-start(), calls=%async_computation.3 | async-start | bytes 4718592 | tf_op jit(solution)/shard_map/all_gather | solution.py:342
  9.2 31.7 %collective-permute-start = (bf16[4,16,32,128]{3,2,1,0:T(8,128)(2,1)}, bf16[4,16,32,128]{3,2,1,0:T(8,128)(2,1)S(1)}, u32[]{:S(2)}, u32[]{:S(2)}) collective-permute-start(bf16[4,16,32,128]{3,2,1,0:T(8,128)(2,1)} %get-tuple-element.14), channel_id=1, source_target_pairs={{0,8},{8,0},{16,24},{24,16},{32,40},{40,32},{48,56},{56,48},{64,72... | collective-permute-start | bytes 1572872 | tf_op jit(solution)/shard_map/ppermute | solution.py:339
  12.6 28.3 %collective-permute-start.1 = (bf16[4,16,32,128]{3,2,1,0:T(8,128)(2,1)}, bf16[4,16,32,128]{3,2,1,0:T(8,128)(2,1)S(1)}, u32[]{:S(2)}, u32[]{:S(2)}) collective-permute-start(bf16[4,16,32,128]{3,2,1,0:T(8,128)(2,1)} %get-tuple-element.15), channel_id=1, source_target_pairs={{0,16},{8,24},{16,0},{24,8},{32,48},{40,56},{48,32},{56,40},{64,80... | collective-permute-start | bytes 1572872 | tf_op jit(solution)/shard_map/ppermute | solution.py:339
  12.6 28.3 %collective-permute-start.2 = (bf16[4,16,32,128]{3,2,1,0:T(8,128)(2,1)}, bf16[4,16,32,128]{3,2,1,0:T(8,128)(2,1)S(1)}, u32[]{:S(2)}, u32[]{:S(2)}) collective-permute-start(bf16[4,16,32,128]{3,2,1,0:T(8,128)(2,1)} %get-tuple-element.16), channel_id=1, source_target_pairs={{0,24},{8,16},{16,8},{24,0},{32,56},{40,48},{48,40},{56,32},{64,88... | collective-permute-start | bytes 1572872 | tf_op jit(solution)/shard_map/ppermute | solution.py:339
  45.5 56.4 %copy-start = (bf16[3,4,448,256]{3,2,1,0:T(8,128)(2,1)S(1)}, bf16[3,4,448,256]{3,2,1,0:T(8,128)(2,1)}, u32[]{:S(2)}) copy-start(bf16[3,4,448,256]{3,2,1,0:T(8,128)(2,1)} %dchi_ref.1) | copy-start | bytes 8257540
  45.5 56.4 %copy-start.1 = (s32[2048]{0:T(1024)S(1)}, s32[2048]{0:T(1024)}, u32[]{:S(2)}) copy-start(s32[2048]{0:T(1024)} %param.13) | copy-start | bytes 24580
  45.5 56.4 %copy-start.2 = (s32[4,16]{1,0:T(4,128)S(1)}, s32[4,16]{1,0:T(4,128)}, u32[]{:S(2)}) copy-start(s32[4,16]{1,0:T(4,128)} %screen_ref.3) | copy-start | bytes 772
Sparse Core Ops, SparseCore 0:
  9.3 58.6 all-gather.2

commit v5 on v4

--- a/solution.py
+++ b/solution.py
@@ -7,7 +7,6 @@
 from jax.experimental.pallas import tpu as pltpu
 from jax.sharding import PartitionSpec as P
 
-PACKED_ROWS = 1024
 MIB = 1024 * 1024
 
 
@@ -16,14 +15,12 @@
     screen_ref,
     grad_ref,
     neighbor_ref,
-    weight_ref,
     *refs,
     group,
-    per_device,
 ):
     outs = refs[:group]
-    packed_ref, weight_out_ref, lists_ref = refs[group : group + 3]
-    held, grad, neighbor, weight, screen, turn, wide, tall, packed, load_sem, sem, small_sem = refs[group + 3 :]
+    packed_ref, lists_ref = refs[group : group + 2]
+    held, grad, neighbor, screen, wide, load_sem, sem, small_sem = refs[group + 2 :]
     part = density_ref.shape[2] // group
     place = lax.rem(lax.axis_index("pts"), group)
     rows = density_ref.shape[0]
@@ -33,16 +30,14 @@
     small = [
         pltpu.make_async_copy(source, target, small_sem.at[i])
         for i, (source, target) in enumerate(
-            [(screen_ref, screen), (grad_ref, grad), (neighbor_ref, neighbor), (weight_ref, weight)]
+            [(screen_ref, screen), (grad_ref, grad), (neighbor_ref, neighbor)]
         )
     ]
     for load in loads:
         load.start()
     for load in small:
         load.start()
-    turn[...] = jnp.full_like(turn, -1.0)
     wide[...] = jnp.full_like(wide, -1.0)
-    tall[...] = jnp.zeros_like(tall)
     copies = []
     for i in range(rows):
         loads[i].wait()
@@ -59,25 +54,32 @@
     for q in range(lists_ref.shape[0]):
         lists_ref[q] = line
     knbr, points = neighbor.shape
-    owner = lax.div(neighbor[...], per_device)
-    inside = neighbor[...] - owner * per_device
     for d in range(3):
         wide[d, :, :points] = grad[d]
-    wide[3, :, :points] = inside.astype(jnp.float32)
+    wide[3, :, :points] = neighbor[...].astype(jnp.float32)
     for c in range(4):
         for h in range(2):
             at = (c * 2 + h) * knbr
-            packed[at : at + knbr, :] = wide[c, :, h * 128 : (h + 1) * 128]
-    turn[:knbr, :points] = owner.astype(jnp.float32)
-    packed[8 * knbr : 8 * knbr + 256, :] = turn[...].T
-    packed_copy = pltpu.make_async_copy(packed, packed_ref.at[pl.ds(0, packed.shape[0])], small_sem.at[4])
-    packed_copy.start()
-    boxes, box_points = weight.shape
-    tall[:boxes, :box_points] = weight[...]
-    weight_out_ref[...] = tall[...].T[:box_points, :]
+            packed_ref[at : at + knbr, :] = wide[c, :, h * 128 : (h + 1) * 128]
     for copy in copies:
         copy.wait()
-    packed_copy.wait()
+
+
+def unpack_kernel(packed_ref, weight_ref, out_ref, weight_out_ref, turn, tall, *, per_device, knbr):
+    turn[...] = jnp.zeros_like(turn)
+    for at in range(packed_ref.shape[0]):
+        out_ref[at, : 6 * knbr, :] = packed_ref[at, : 6 * knbr, :]
+        for h in range(2):
+            rows = slice((6 + h) * knbr, (7 + h) * knbr)
+            atoms = packed_ref[at, rows, :].astype(jnp.int32)
+            owner = lax.div(atoms, per_device)
+            out_ref[at, rows, :] = (atoms - owner * per_device).astype(jnp.float32)
+            turn[at, :knbr, h * 128 : (h + 1) * 128] = owner.astype(jnp.float32)
+        out_ref[at, 8 * knbr :, :] = turn[at].T
+    tall[...] = jnp.zeros_like(tall)
+    boxes, box_points = weight_ref.shape
+    tall[:boxes, :box_points] = weight_ref[...]
+    weight_out_ref[...] = tall[...].T[:box_points, :]
 
 
 def send_kernel(lists_ref, *refs, boxes, slots, own):
@@ -169,7 +171,7 @@
     devices = out_ref.shape[0]
 
     packed_copy = pltpu.make_async_copy(
-        packed_ref.at[:, pl.ds(0, packed_buf.shape[1])], packed_buf, packed_sem
+        packed_ref, packed_buf, packed_sem
     )
     columns = [[screen_ref[x, bas * own + j] - bas * span for j in range(own)] for x in range(boxes)]
 
@@ -309,37 +311,46 @@
     vmem = pl.BlockSpec(memory_space=pltpu.VMEM)
 
     group = n_pts // n_bas
-    *pieces, packed, weight_lines, flat = pl.pallas_call(
-        functools.partial(first_kernel, group=group, per_device=per_device),
+    *pieces, packed, flat = pl.pallas_call(
+        functools.partial(first_kernel, group=group),
         out_shape=[pltpu.HBM((rows, span, block // group, block), density.dtype)] * group
         + [
-            pltpu.HBM((PACKED_ROWS, 128), jnp.float32),
-            jax.ShapeDtypeStruct((points, 128), jnp.float32),
+            jax.ShapeDtypeStruct((8 * knbr, 128), jnp.float32),
             jax.ShapeDtypeStruct((n_pts, 1, boxes * slots), jnp.int32),
         ],
-        in_specs=[hbm] * 5,
-        out_specs=[hbm] * (group + 1) + [vmem] * 2,
+        in_specs=[hbm] * 4,
+        out_specs=[hbm] * group + [vmem] * 2,
         scratch_shapes=[
             pltpu.VMEM(density.shape, density.dtype),
             pltpu.VMEM(weight_grad.shape, jnp.float32),
             pltpu.VMEM(neighbors.shape, jnp.int32),
-            pltpu.VMEM(weights.shape, jnp.float32),
             pltpu.VMEM(screen.shape, jnp.int32),
-            pltpu.VMEM((128, 256), jnp.float32),
             pltpu.VMEM((4, knbr, 256), jnp.float32),
-            pltpu.VMEM((128, 512), jnp.float32),
-            pltpu.VMEM((8 * knbr + 256, 128), jnp.float32),
             pltpu.SemaphoreType.DMA((rows,)),
             pltpu.SemaphoreType.DMA((group, rows)),
-            pltpu.SemaphoreType.DMA((5,)),
+            pltpu.SemaphoreType.DMA((3,)),
         ],
         compiler_params=pltpu.CompilerParams(vmem_limit_bytes=12 * MIB),
-    )(in_hbm(density), in_hbm(screen), in_hbm(weight_grad), in_hbm(neighbors), in_hbm(weights))
+    )(in_hbm(density), in_hbm(screen), in_hbm(weight_grad), in_hbm(neighbors))
     pieces = [in_hbm(pieces[0])] + [
         lax.ppermute(pieces[d], "pts", [(p, p ^ d) for p in range(n_pts)]) for d in range(1, group)
     ]
     lists = lax.all_to_all(flat, "pts", split_axis=0, concat_axis=0, tiled=True)
-    gathered = in_hbm(lax.all_gather(packed, "bas", axis=0))
+    unpacked, weight_lines = pl.pallas_call(
+        functools.partial(unpack_kernel, per_device=per_device, knbr=knbr),
+        out_shape=(
+            jax.ShapeDtypeStruct((n_bas, 8 * knbr + 256, 128), jnp.float32),
+            jax.ShapeDtypeStruct((points, 128), jnp.float32),
+        ),
+        in_specs=[vmem] * 2,
+        out_specs=(vmem, vmem),
+        scratch_shapes=[
+            pltpu.VMEM((n_bas, 128, 256), jnp.float32),
+            pltpu.VMEM((128, 512), jnp.float32),
+        ],
+        compiler_params=pltpu.CompilerParams(vmem_limit_bytes=12 * MIB),
+        cost_estimate=pl.CostEstimate(flops=5_000_000, bytes_accessed=4_000_000, transcendentals=0),
+    )(lax.all_gather(packed, "bas", axis=0), weights)
     outgoing = pl.pallas_call(
         functools.partial(send_kernel, boxes=boxes, slots=slots, own=own),
         out_shape=pltpu.HBM((n_pts, boxes * own, block // group, own * block), density.dtype),
@@ -363,7 +374,7 @@
         in_hbm(arrived),
         weight_lines,
         basis_atom.reshape(span, block),
-        gathered,
+        in_hbm(unpacked),
         devices,
         per_device,
     )

time: 144 us -> 132 us (0.917)
  blocking collectives: 107 us -> 77.4 us
  waiting for transfers between devices: 0.03 us -> 23.9 us
  between operations: 13.4 us -> 0.09 us
  starting transfers between devices: 5.06 us -> 10.4 us
    all_to_all x1 -> x0, blocking collectives: 56.4 us -> none  [shards(): lax.all_to_all(outgoing, 'pts', split_axis=0, concat_axis=0, tiled=True)]
    all_gather x0 -> x1, blocking collectives: none -> 24.9 us  [shards(): lax.all_gather(packed, 'bas', axis=0)]
    all_to_all x0 -> x1, waiting for transfers between devices: none -> 23.9 us  [shards(): lax.all_to_all(outgoing, 'pts', split_axis=0, concat_axis=0, tiled=True)]
    all_to_all x0 -> x1, starting transfers between devices: none -> 5.36 us  [shards(): lax.all_to_all(outgoing, 'pts', split_axis=0, concat_axis=0, tiled=True)]
    all_to_all x1, blocking collectives: 24.5 us -> 26 us  [shards(): lax.all_to_all(parts, ('pts', 'bas'), split_axis=0, concat_axis=0, tiled=...]
    pallas_call x1 -> x2, Pallas kernels: 2.65 us -> 2.96 us  [the longest x1 2.55 us: shards(): pl.pallas_call(functools.partial(first_kernel, group=group), out_shape=[p...]
  transfers between devices with their start and end apart: 4 -> 4, of which waited for: 0 -> 1; matrix products, arithmetic and copies ran while one was open for 0% -> 0% of each run, Pallas kernels for 3% -> 0%
where the time goes in v5:
time: 132 us; the launch traced here: 131 us
  blocking collectives  77.4 us (59%)
  waiting for transfers between devices  23.9 us (18%)
  Pallas kernels  17.4 us (13%)
  starting transfers between devices  10.4 us (8%)
  local copies, waits for them, and re-layouts  1.85 us (1%)
    all_to_all x1, blocking collectives, shards(): lists = lax.all_to_all(flat, 'pts', split_axis=0, concat_axis=0, tiled=True)  26.6 us
    all_to_all x1, blocking collectives, shards(): lax.all_to_all(parts, ('pts', 'bas'), split_axis=0, concat_axis=0, tiled=...  26 us
    all_gather x1, blocking collectives, shards(): lax.all_gather(packed, 'bas', axis=0)  24.9 us
    all_to_all x1, waiting for transfers between devices, shards(): lax.all_to_all(outgoing, 'pts', split_axis=0, concat_axis=0, tiled=True)  23.9 us
    pallas_call x1, Pallas kernels, run_main(): pl.pallas_call(functools.partial(main_kernel, per_device=per_device, knbr...  9.88 us
    all_to_all x1, starting transfers between devices, shards(): lax.all_to_all(outgoing, 'pts', split_axis=0, concat_axis=0, tiled=True)  5.36 us
    ppermute x3, starting transfers between devices, shards(): lax.ppermute(pieces[d], 'pts', [(p, p ^ d) for p in range(n_pts)])  5.06 us
    pallas_call x1, Pallas kernels, shards(): pl.pallas_call(functools.partial(send_kernel, boxes=boxes, slots=slots, o...  4.53 us
  transfers between devices with their start and end apart: 4, of which 1 were waited for; matrix products, arithmetic and copies ran while one was open for 0% of the time, Pallas kernels for 0%

profile of v5, /device:TPU:1, one launch (start us, length us, event | category | flops | bytes accessed | tf_op | source)
XLA Modules:
  0.0 131.4 jit_solution(6951210445564567994)
XLA Ops:
  0.0 2.5 %shard_map.82 = (bf16[4,16,32,128]{3,2,1,0:T(8,128)(2,1)}, bf16[4,16,32,128]{3,2,1,0:T(8,128)(2,1)}, bf16[4,16,32,128]{3,2,1,0:T(8,128)(2,1)}, bf16[4,16,32,128]...) custom-call(bf16[4,16,128,128]{3,2,1,0:T(8,128)(2,1)} %density_ref.1, s32[4,16]{1,0:T(4,128)} %screen_ref.3, ...), custom_call_target="tpu_custom_call" | custom-call | tf_op jit(solution)/shard_map/pallas_call | solution.py:314
  2.6 3.3 %collective-permute-start = (bf16[4,16,32,128]{3,2,1,0:T(8,128)(2,1)}, bf16[4,16,32,128]{3,2,1,0:T(8,128)(2,1)S(1)}, u32[]{:S(2)}, u32[]{:S(2)}) collective-permute-start(bf16[4,16,32,128]{3,2,1,0:T(8,128)(2,1)} %get-tuple-element.15), channel_id=1, source_target_pairs={{0,8},{8,0},{16,24},{24,16},{32,40},{40,32},{48,56},{56,48},{64,72... | collective-permute-start | bytes 1572872 | tf_op jit(solution)/shard_map/ppermute | solution.py:336
  5.9 0.0 collective-permute-start.1
  5.9 1.7 %collective-permute-start.2 = (bf16[4,16,32,128]{3,2,1,0:T(8,128)(2,1)}, bf16[4,16,32,128]{3,2,1,0:T(8,128)(2,1)S(1)}, u32[]{:S(2)}, u32[]{:S(2)}) collective-permute-start(bf16[4,16,32,128]{3,2,1,0:T(8,128)(2,1)} %get-tuple-element.17), channel_id=1, source_target_pairs={{0,24},{8,16},{16,8},{24,0},{32,56},{40,48},{48,40},{56,32},{64,88... | collective-permute-start | bytes 1572872 | tf_op jit(solution)/shard_map/ppermute | solution.py:336
  7.6 26.6 %all_to_all.15.lists_ref = s32[32,1,64]{2,1,0:T(1,128)S(1)} all-to-all(s32[32,1,64]{2,1,0:T(1,128)S(1)} %get-tuple-element.13), channel_id=1, replica_groups=mesh['pts'=32,'bas'=8] {'pts'}, dimensions={0} | all-to-all | bytes 16384 | tf_op jit(solution)/shard_map/all_to_all | solution.py:338
  34.2 0.0 collective-permute-done.refs_1_
  34.2 0.0 collective-permute-done.1.refs_2_
  34.2 0.0 collective-permute-done.2.refs_3_
  34.2 4.5 %shard_map.83 = bf16[32,8,32,256]{3,2,1,0:T(8,128)(2,1)} custom-call(s32[32,1,64]{2,1,0:T(1,128)S(1)} %all_to_all.15.lists_ref, bf16[4,16,32,128]{3,2,1,0:T(8,128)(2,1)} %get-tuple-element.14.refs_0_, bf16[4,16,32,128]{3,2,1,0:T(8,128)(2,1)S(1)} %collective-permute-done.refs_1_, bf16[4,16,32,128]{3,2,1,0:T(8,128)(2,1)S(1)} %collective-permute-done.1.refs_2_, ...), custom_call_target="tpu_custom_call" | custom-call | tf_op jit(solution)/shard_map/pallas_call | solution.py:354
  38.8 0.0 copy-start.3
  38.8 0.0 copy-start
  38.8 0.0 copy-start.2
  38.8 0.0 copy-start.4
  38.8 5.4 %all-to-all-start.1 = ((bf16[32,8,32,256]{3,2,1,0:T(8,128)(2,1)}), bf16[32,8,32,256]{3,2,1,0:T(8,128)(2,1)}, u32[]{:S(2)}, u32[]{:S(2)}) async-start(bf16[32,8,32,256]{3,2,1,0:T(8,128)(2,1)} %shard_map.83), calls=%async_computation.1 | async-start | bytes 8388608 | tf_op jit(solution)/shard_map/all_to_all | solution.py:367
  44.2 24.9 %all-gather = f32[512,128]{1,0:T(8,128)S(1)} all-gather(f32[64,128]{1,0:T(8,128)S(1)} %get-tuple-element.18), channel_id=2, replica_groups=mesh['pts'=32,'bas'=8] {'bas'}, dimensions={0}, use_global_device_ids=true | all-gather | bytes 294912 | tf_op jit(solution)/shard_map/all_gather | solution.py:353
  69.0 0.0 copy-done.3
  69.0 0.4 shard_map.84
  69.5 0.0 copy-start.1
  69.5 1.2 copy-done.1
  70.6 23.9 %all-to-all-done.1 = bf16[32,8,32,256]{3,2,1,0:T(8,128)(2,1)} async-done(((bf16[32,8,32,256]{3,2,1,0:T(8,128)(2,1)}), bf16[32,8,32,256]{3,2,1,0:T(8,128)(2,1)}, u32[]{:S(2)}, u32[]{:S(2)}) %all-to-all-start.1) | async-done | bytes 4194336 | tf_op jit(solution)/shard_map/all_to_all | solution.py:367
  94.6 0.0 copy-done
  94.6 0.0 copy-done.2
  94.6 0.0 copy-done.4
  94.6 9.9 %shard_map.85 = f32[256,128]{1,0:T(8,128)S(1)} custom-call(s32[4,16]{1,0:T(4,128)S(1)} %copy-done.4, bf16[4,448,2048]{2,1,0:T(8,128)(2,1)} %chi_ref.1, bf16[3,4,448,256]{3,2,1,0:T(8,128)(2,1)S(1)} %copy-done, bf16[8,4,8,32,256]{4,3,2,1,0:T(8,128)(2,1)} %bitcast.arrived_ref, f32[448,128]{1,0:T(8,128)S(1)} %get-tuple-element.19.weight_ref, ...), custom_call_target="tpu_custom_call" | custom-call | flops 2000000000 | bytes 30000000 | tf_op jit(solution)/shard_map/pallas_call | solution.py:272
  104.5 26.0 %all_to_all.16 = f32[256,1,36]{2,1,0:T(1,128)S(1)} all-to-all(f32[256,1,36]{2,1,0:T(1,128)S(1)} %bitcast.8), channel_id=1, replica_groups=mesh['pts'=32,'bas'=8] {'pts','bas'}, dimensions={0} | all-to-all | bytes 73728 | tf_op jit(solution)/shard_map/all_to_all | solution.py:382
  130.4 0.3 reduce_sum.9
  130.7 0.7 reshape.15
Async XLA Ops:
  2.6 31.7 %collective-permute-start = (bf16[4,16,32,128]{3,2,1,0:T(8,128)(2,1)}, bf16[4,16,32,128]{3,2,1,0:T(8,128)(2,1)S(1)}, u32[]{:S(2)}, u32[]{:S(2)}) collective-permute-start(bf16[4,16,32,128]{3,2,1,0:T(8,128)(2,1)} %get-tuple-element.15), channel_id=1, source_target_pairs={{0,8},{8,0},{16,24},{24,16},{32,40},{40,32},{48,56},{56,48},{64,72... | collective-permute-start | bytes 1572872 | tf_op jit(solution)/shard_map/ppermute | solution.py:336
  5.9 28.3 %collective-permute-start.1 = (bf16[4,16,32,128]{3,2,1,0:T(8,128)(2,1)}, bf16[4,16,32,128]{3,2,1,0:T(8,128)(2,1)S(1)}, u32[]{:S(2)}, u32[]{:S(2)}) collective-permute-start(bf16[4,16,32,128]{3,2,1,0:T(8,128)(2,1)} %get-tuple-element.16), channel_id=1, source_target_pairs={{0,16},{8,24},{16,0},{24,8},{32,48},{40,56},{48,32},{56,40},{64,80... | collective-permute-start | bytes 1572872 | tf_op jit(solution)/shard_map/ppermute | solution.py:336
  5.9 28.3 %collective-permute-start.2 = (bf16[4,16,32,128]{3,2,1,0:T(8,128)(2,1)}, bf16[4,16,32,128]{3,2,1,0:T(8,128)(2,1)S(1)}, u32[]{:S(2)}, u32[]{:S(2)}) collective-permute-start(bf16[4,16,32,128]{3,2,1,0:T(8,128)(2,1)} %get-tuple-element.17), channel_id=1, source_target_pairs={{0,24},{8,16},{16,8},{24,0},{32,56},{40,48},{48,40},{56,32},{64,88... | collective-permute-start | bytes 1572872 | tf_op jit(solution)/shard_map/ppermute | solution.py:336
  38.8 30.3 %copy-start.3 = (f32[4,448]{1,0:T(4,128)S(1)}, f32[4,448]{1,0:T(4,128)}, u32[]{:S(2)}) copy-start(f32[4,448]{1,0:T(4,128)} %weight_ref.1) | copy-start | bytes 21508
  38.8 55.8 %copy-start = (bf16[3,4,448,256]{3,2,1,0:T(8,128)(2,1)S(1)}, bf16[3,4,448,256]{3,2,1,0:T(8,128)(2,1)}, u32[]{:S(2)}) copy-start(bf16[3,4,448,256]{3,2,1,0:T(8,128)(2,1)} %dchi_ref.1) | copy-start | bytes 8257540
  38.8 55.8 %copy-start.2 = (s32[2048]{0:T(1024)S(1)}, s32[2048]{0:T(1024)}, u32[]{:S(2)}) copy-start(s32[2048]{0:T(1024)} %param.13) | copy-start | bytes 24580
  38.8 55.8 %copy-start.4 = (s32[4,16]{1,0:T(4,128)S(1)}, s32[4,16]{1,0:T(4,128)}, u32[]{:S(2)}) copy-start(s32[4,16]{1,0:T(4,128)} %screen_ref.3) | copy-start | bytes 772
  38.8 55.7 %all-to-all-start.1 = ((bf16[32,8,32,256]{3,2,1,0:T(8,128)(2,1)}), bf16[32,8,32,256]{3,2,1,0:T(8,128)(2,1)}, u32[]{:S(2)}, u32[]{:S(2)}) async-start(bf16[32,8,32,256]{3,2,1,0:T(8,128)(2,1)} %shard_map.83), calls=%async_computation.1 | async-start | bytes 8388608 | tf_op jit(solution)/shard_map/all_to_all | solution.py:367
  69.5 1.2 copy-start.1

commit v6 on v5

--- a/solution.py
+++ b/solution.py
@@ -82,8 +82,10 @@
     weight_out_ref[...] = tall[...].T[:box_points, :]
 
 
-def send_kernel(lists_ref, *refs, boxes, slots, own):
-    *pieces, out_ref, held, stage, load_sem, sem = refs
+def send_kernel(lists_hbm, *refs, boxes, slots, own):
+    *pieces, out_ref, lists_ref, held, stage, lists_sem, load_sem, sem = refs
+    lists_load = pltpu.make_async_copy(lists_hbm, lists_ref, lists_sem)
+    lists_load.start()
     group = len(pieces)
     rows, span = pieces[0].shape[:2]
     block = held.shape[-1]
@@ -96,6 +98,7 @@
         start = jnp.bitwise_xor(place, d) * rows
         loads.append(pltpu.make_async_copy(piece, held.at[pl.ds(start, rows)], load_sem.at[d]))
         loads[-1].start()
+    lists_load.wait()
     for load in loads:
         load.wait()
 
@@ -111,7 +114,7 @@
         pltpu.make_async_copy(stage.at[q], out_ref.at[q], sem).start()
         return carry
 
-    lax.fori_loop(0, lists_ref.shape[0], one_index, 0, unroll=2)
+    lax.fori_loop(0, lists_ref.shape[0], one_index, 0, unroll=8)
     pltpu.make_async_copy(stage, out_ref, sem).wait()
 
 
@@ -141,7 +144,7 @@
 
 
 def main_kernel(
-    screen_ref,
+    screen_hbm,
     chi_ref,
     dchi_ref,
     arrived_ref,
@@ -153,6 +156,8 @@
     block_buf,
     packed_buf,
     turn,
+    screen_ref,
+    screen_sem,
     chi_sem,
     block_sem,
     packed_sem,
@@ -173,7 +178,8 @@
     packed_copy = pltpu.make_async_copy(
         packed_ref, packed_buf, packed_sem
     )
-    columns = [[screen_ref[x, bas * own + j] - bas * span for j in range(own)] for x in range(boxes)]
+    screen_copy = pltpu.make_async_copy(screen_hbm, screen_ref, screen_sem)
+    screen_copy.start()
 
     def block_copies(x):
         for t in range(own):
@@ -188,6 +194,8 @@
         chi_copy(x).start()
         block_copies(x)
     packed_copy.start()
+    screen_copy.wait()
+    columns = [[screen_ref[x, bas * own + j] - bas * span for j in range(own)] for x in range(boxes)]
 
     owner_lane = lax.broadcasted_iota(jnp.int32, (1, devices), 1).astype(jnp.float32).astype(jnp.bfloat16)
     one = jnp.ones((), jnp.bfloat16)
@@ -266,19 +274,20 @@
     n_bas = lax.axis_size("bas")
     knbr = 8
     hbm = pl.BlockSpec(memory_space=pltpu.HBM)
-    smem = pl.BlockSpec(memory_space=pltpu.SMEM)
     vmem = pl.BlockSpec(memory_space=pltpu.VMEM)
     ranges, group, asked, part, width = arrived.shape
     return pl.pallas_call(
         functools.partial(main_kernel, per_device=per_device, knbr=knbr),
         out_shape=jax.ShapeDtypeStruct((devices, 128), jnp.float32),
-        in_specs=[smem, hbm, vmem, hbm, vmem, vmem, hbm],
+        in_specs=[hbm, hbm, vmem, hbm, vmem, vmem, hbm],
         out_specs=vmem,
         scratch_shapes=[
             pltpu.VMEM(chi.shape, chi.dtype),
             pltpu.VMEM((boxes, ranges, asked // boxes, group, part, width), arrived.dtype),
             pltpu.VMEM((n_bas, 8 * knbr + 256, 128), jnp.float32),
             pltpu.VMEM((256, 128), jnp.float32),
+            pltpu.SMEM(screen.shape, jnp.int32),
+            pltpu.SemaphoreType.DMA,
             pltpu.SemaphoreType.DMA((boxes,)),
             pltpu.SemaphoreType.DMA((boxes,)),
             pltpu.SemaphoreType.DMA,
@@ -307,7 +316,6 @@
     knbr = neighbors.shape[0]
     per_device = 12
     hbm = pl.BlockSpec(memory_space=pltpu.HBM)
-    smem = pl.BlockSpec(memory_space=pltpu.SMEM)
     vmem = pl.BlockSpec(memory_space=pltpu.VMEM)
 
     group = n_pts // n_bas
@@ -354,11 +362,13 @@
     outgoing = pl.pallas_call(
         functools.partial(send_kernel, boxes=boxes, slots=slots, own=own),
         out_shape=pltpu.HBM((n_pts, boxes * own, block // group, own * block), density.dtype),
-        in_specs=[smem] + [hbm] * group,
+        in_specs=[hbm] * (group + 1),
         out_specs=hbm,
         scratch_shapes=[
+            pltpu.SMEM(lists.shape, jnp.int32),
             pltpu.VMEM((group * rows, span, block // group, block), density.dtype),
             pltpu.VMEM((n_pts, boxes * own, block // group, own * block), density.dtype),
+            pltpu.SemaphoreType.DMA,
             pltpu.SemaphoreType.DMA((group,)),
             pltpu.SemaphoreType.DMA,
         ],
@@ -368,7 +378,7 @@
     arrived = arrived.reshape(n_bas, group, boxes * own, block // group, own * block)
 
     parts = run_main(
-        screen,
+        in_hbm(screen),
         in_hbm(chi),
         dchi,
         in_hbm(arrived),

time: 132 us -> 130 us (0.985)
  Pallas kernels: 17.4 us -> 15.7 us
where the time goes in v6:
time: 130 us
  blocking collectives  77.4 us (60%)
  waiting for transfers between devices  24 us (18%)
  Pallas kernels  15.7 us (12%)
  starting transfers between devices  10.4 us (8%)
  local copies, waits for them, and re-layouts  1.81 us (1%)
    all_to_all x1, blocking collectives, shards(): lists = lax.all_to_all(flat, 'pts', split_axis=0, concat_axis=0, tiled=True)  26.6 us
    all_to_all x1, blocking collectives, shards(): lax.all_to_all(parts, ('pts', 'bas'), split_axis=0, concat_axis=0, tiled=...  26 us
    all_gather x1, blocking collectives, shards(): lax.all_gather(packed, 'bas', axis=0)  24.9 us
    all_to_all x1, waiting for transfers between devices, shards(): lax.all_to_all(outgoing, 'pts', split_axis=0, concat_axis=0, tiled=True)  24 us
    pallas_call x1, Pallas kernels, run_main(): pl.pallas_call(functools.partial(main_kernel, per_device=per_device, knbr...  9.32 us
    all_to_all x1, starting transfers between devices, shards(): lax.all_to_all(outgoing, 'pts', split_axis=0, concat_axis=0, tiled=True)  5.36 us
    ppermute x3, starting transfers between devices, shards(): lax.ppermute(pieces[d], 'pts', [(p, p ^ d) for p in range(n_pts)])  5.06 us
    pallas_call x1, Pallas kernels, shards(): pl.pallas_call(functools.partial(send_kernel, boxes=boxes, slots=slots, o...  3.46 us
  transfers between devices with their start and end apart: 4, of which 1 were waited for; matrix products, arithmetic and copies ran while one was open for 0% of the time, Pallas kernels for 0%

profile of v6, /device:TPU:1, one launch (start us, length us, event | category | flops | bytes accessed | tf_op | source)
XLA Modules:
  0.0 129.7 jit_solution(8287652866632624879)
XLA Ops:
  0.0 2.5 %shard_map.82 = (bf16[4,16,32,128]{3,2,1,0:T(8,128)(2,1)}, bf16[4,16,32,128]{3,2,1,0:T(8,128)(2,1)}, bf16[4,16,32,128]{3,2,1,0:T(8,128)(2,1)}, bf16[4,16,32,128]...) custom-call(bf16[4,16,128,128]{3,2,1,0:T(8,128)(2,1)} %density_ref.1, s32[4,16]{1,0:T(4,128)} %screen_hbm.1, ...), custom_call_target="tpu_custom_call" | custom-call | tf_op jit(solution)/shard_map/pallas_call | solution.py:322
  2.5 3.3 %collective-permute-start = (bf16[4,16,32,128]{3,2,1,0:T(8,128)(2,1)}, bf16[4,16,32,128]{3,2,1,0:T(8,128)(2,1)S(1)}, u32[]{:S(2)}, u32[]{:S(2)}) collective-permute-start(bf16[4,16,32,128]{3,2,1,0:T(8,128)(2,1)} %get-tuple-element.15), channel_id=1, source_target_pairs={{0,8},{8,0},{16,24},{24,16},{32,40},{40,32},{48,56},{56,48},{64,72... | collective-permute-start | bytes 1572872 | tf_op jit(solution)/shard_map/ppermute | solution.py:344
  5.9 0.0 collective-permute-start.1
  5.9 1.7 %collective-permute-start.2 = (bf16[4,16,32,128]{3,2,1,0:T(8,128)(2,1)}, bf16[4,16,32,128]{3,2,1,0:T(8,128)(2,1)S(1)}, u32[]{:S(2)}, u32[]{:S(2)}) collective-permute-start(bf16[4,16,32,128]{3,2,1,0:T(8,128)(2,1)} %get-tuple-element.17), channel_id=1, source_target_pairs={{0,24},{8,16},{16,8},{24,0},{32,56},{40,48},{48,40},{56,32},{64,88... | collective-permute-start | bytes 1572872 | tf_op jit(solution)/shard_map/ppermute | solution.py:344
  7.6 26.6 %all_to_all.15.lists_hbm = s32[32,1,64]{2,1,0:T(1,128)S(1)} all-to-all(s32[32,1,64]{2,1,0:T(1,128)S(1)} %get-tuple-element.13), channel_id=1, replica_groups=mesh['pts'=32,'bas'=8] {'pts'}, dimensions={0} | all-to-all | bytes 16384 | tf_op jit(solution)/shard_map/all_to_all | solution.py:346
  34.2 0.0 collective-permute-done.refs_1_
  34.2 0.0 collective-permute-done.1.refs_2_
  34.2 0.0 collective-permute-done.2.refs_3_
  34.2 3.5 %shard_map.83 = bf16[32,8,32,256]{3,2,1,0:T(8,128)(2,1)} custom-call(s32[32,1,64]{2,1,0:T(1,128)S(1)} %all_to_all.15.lists_hbm, bf16[4,16,32,128]{3,2,1,0:T(8,128)(2,1)} %get-tuple-element.14.refs_0_, bf16[4,16,32,128]{3,2,1,0:T(8,128)(2,1)S(1)} %collective-permute-done.refs_1_, bf16[4,16,32,128]{3,2,1,0:T(8,128)(2,1)S(1)} %collective-permute-done.1.refs_2_, ...), custom_call_target="tpu_custom_call" | custom-call | tf_op jit(solution)/shard_map/pallas_call | solution.py:362
  37.7 0.0 copy-start.3
  37.7 0.0 copy-start
  37.7 0.0 copy-start.2
  37.7 5.4 %all-to-all-start.1 = ((bf16[32,8,32,256]{3,2,1,0:T(8,128)(2,1)}), bf16[32,8,32,256]{3,2,1,0:T(8,128)(2,1)}, u32[]{:S(2)}, u32[]{:S(2)}) async-start(bf16[32,8,32,256]{3,2,1,0:T(8,128)(2,1)} %shard_map.83), calls=%async_computation.1 | async-start | bytes 8388608 | tf_op jit(solution)/shard_map/all_to_all | solution.py:377
  43.1 24.9 %all-gather = f32[512,128]{1,0:T(8,128)S(1)} all-gather(f32[64,128]{1,0:T(8,128)S(1)} %get-tuple-element.18), channel_id=2, replica_groups=mesh['pts'=32,'bas'=8] {'bas'}, dimensions={0}, use_global_device_ids=true | all-gather | bytes 294912 | tf_op jit(solution)/shard_map/all_gather | solution.py:361
  68.0 0.0 copy-done.3
  68.0 0.4 shard_map.84
  68.4 0.0 copy-start.1
  68.4 1.1 copy-done.1
  69.5 24.0 %all-to-all-done.1 = bf16[32,8,32,256]{3,2,1,0:T(8,128)(2,1)} async-done(((bf16[32,8,32,256]{3,2,1,0:T(8,128)(2,1)}), bf16[32,8,32,256]{3,2,1,0:T(8,128)(2,1)}, u32[]{:S(2)}, u32[]{:S(2)}) %all-to-all-start.1) | async-done | bytes 4194336 | tf_op jit(solution)/shard_map/all_to_all | solution.py:377
  93.5 0.0 copy-done
  93.5 0.0 copy-done.2
  93.5 9.3 %shard_map.85 = f32[256,128]{1,0:T(8,128)S(1)} custom-call(s32[4,16]{1,0:T(4,128)} %screen_hbm.1, bf16[4,448,2048]{2,1,0:T(8,128)(2,1)} %chi_ref.1, bf16[3,4,448,256]{3,2,1,0:T(8,128)(2,1)S(1)} %copy-done, bf16[8,4,8,32,256]{4,3,2,1,0:T(8,128)(2,1)} %bitcast.arrived_ref, f32[448,128]{1,0:T(8,128)S(1)} %get-tuple-element.19.weight_ref, ...), custom_call_target="tpu_custom_call" | custom-call | flops 2000000000 | bytes 30000000 | tf_op jit(solution)/shard_map/pallas_call | solution.py:279
  102.8 26.0 %all_to_all.16 = f32[256,1,36]{2,1,0:T(1,128)S(1)} all-to-all(f32[256,1,36]{2,1,0:T(1,128)S(1)} %bitcast.8), channel_id=1, replica_groups=mesh['pts'=32,'bas'=8] {'pts','bas'}, dimensions={0} | all-to-all | bytes 73728 | tf_op jit(solution)/shard_map/all_to_all | solution.py:392
  128.8 0.3 reduce_sum.9
  129.1 0.7 reshape.15
Async XLA Ops:
  2.5 31.7 %collective-permute-start = (bf16[4,16,32,128]{3,2,1,0:T(8,128)(2,1)}, bf16[4,16,32,128]{3,2,1,0:T(8,128)(2,1)S(1)}, u32[]{:S(2)}, u32[]{:S(2)}) collective-permute-start(bf16[4,16,32,128]{3,2,1,0:T(8,128)(2,1)} %get-tuple-element.15), channel_id=1, source_target_pairs={{0,8},{8,0},{16,24},{24,16},{32,40},{40,32},{48,56},{56,48},{64,72... | collective-permute-start | bytes 1572872 | tf_op jit(solution)/shard_map/ppermute | solution.py:344
  5.9 28.3 %collective-permute-start.1 = (bf16[4,16,32,128]{3,2,1,0:T(8,128)(2,1)}, bf16[4,16,32,128]{3,2,1,0:T(8,128)(2,1)S(1)}, u32[]{:S(2)}, u32[]{:S(2)}) collective-permute-start(bf16[4,16,32,128]{3,2,1,0:T(8,128)(2,1)} %get-tuple-element.16), channel_id=1, source_target_pairs={{0,16},{8,24},{16,0},{24,8},{32,48},{40,56},{48,32},{56,40},{64,80... | collective-permute-start | bytes 1572872 | tf_op jit(solution)/shard_map/ppermute | solution.py:344
  5.9 28.3 %collective-permute-start.2 = (bf16[4,16,32,128]{3,2,1,0:T(8,128)(2,1)}, bf16[4,16,32,128]{3,2,1,0:T(8,128)(2,1)S(1)}, u32[]{:S(2)}, u32[]{:S(2)}) collective-permute-start(bf16[4,16,32,128]{3,2,1,0:T(8,128)(2,1)} %get-tuple-element.17), channel_id=1, source_target_pairs={{0,24},{8,16},{16,8},{24,0},{32,56},{40,48},{48,40},{56,32},{64,88... | collective-permute-start | bytes 1572872 | tf_op jit(solution)/shard_map/ppermute | solution.py:344
  37.7 30.3 %copy-start.3 = (f32[4,448]{1,0:T(4,128)S(1)}, f32[4,448]{1,0:T(4,128)}, u32[]{:S(2)}) copy-start(f32[4,448]{1,0:T(4,128)} %weight_ref.1) | copy-start | bytes 21508
  37.7 55.8 %copy-start = (bf16[3,4,448,256]{3,2,1,0:T(8,128)(2,1)S(1)}, bf16[3,4,448,256]{3,2,1,0:T(8,128)(2,1)}, u32[]{:S(2)}) copy-start(bf16[3,4,448,256]{3,2,1,0:T(8,128)(2,1)} %dchi_ref.1) | copy-start | bytes 8257540
  37.7 55.8 %copy-start.2 = (s32[2048]{0:T(1024)S(1)}, s32[2048]{0:T(1024)}, u32[]{:S(2)}) copy-start(s32[2048]{0:T(1024)} %param.13) | copy-start | bytes 24580
  37.7 55.8 %all-to-all-start.1 = ((bf16[32,8,32,256]{3,2,1,0:T(8,128)(2,1)}), bf16[32,8,32,256]{3,2,1,0:T(8,128)(2,1)}, u32[]{:S(2)}, u32[]{:S(2)}) async-start(bf16[32,8,32,256]{3,2,1,0:T(8,128)(2,1)} %shard_map.83), calls=%async_computation.1 | async-start | bytes 8388608 | tf_op jit(solution)/shard_map/all_to_all | solution.py:377
  68.4 1.1 copy-start.1

commit v7 on v6

--- a/solution.py
+++ b/solution.py
@@ -116,6 +116,13 @@
 
     lax.fori_loop(0, lists_ref.shape[0], one_index, 0, unroll=8)
     pltpu.make_async_copy(stage, out_ref, sem).wait()
+
+
+def sum_kernel(parts_ref, out_ref):
+    per_device = out_ref.shape[1]
+    total = jnp.sum(parts_ref[...], axis=0, keepdims=True)
+    for d in range(3):
+        out_ref[d : d + 1, :] = total[:, d * per_device : (d + 1) * per_device]
 
 
 def in_hbm(array):
@@ -390,7 +397,13 @@
     )
     parts = parts[:, : 3 * per_device].reshape(devices, 1, 3 * per_device)
     parts = lax.all_to_all(parts, ("pts", "bas"), split_axis=0, concat_axis=0, tiled=True)
-    return jnp.sum(parts, axis=(0, 1)).reshape(3, per_device)
+    return pl.pallas_call(
+        sum_kernel,
+        out_shape=jax.ShapeDtypeStruct((3, per_device), jnp.float32),
+        in_specs=[vmem],
+        out_specs=vmem,
+        compiler_params=pltpu.CompilerParams(vmem_limit_bytes=4 * MIB),
+    )(parts.reshape(devices, 3 * per_device))
 
 
 def solution(mesh):

time: 130 us -> 130 us (level)
  no operation moved by 1% of the time
where the time goes in v7:
time: 130 us; the launch traced here: 129 us
  blocking collectives  77.4 us (60%)
  waiting for transfers between devices  23.9 us (18%)
  Pallas kernels  16.4 us (13%)
  starting transfers between devices  10.4 us (8%)
    all_to_all x1, blocking collectives, shards(): lists = lax.all_to_all(flat, 'pts', split_axis=0, concat_axis=0, tiled=True)  26.6 us
    all_to_all x1, blocking collectives, shards(): lax.all_to_all(parts, ('pts', 'bas'), split_axis=0, concat_axis=0, tiled=...  26 us
    all_gather x1, blocking collectives, shards(): lax.all_gather(packed, 'bas', axis=0)  24.9 us
    all_to_all x1, waiting for transfers between devices, shards(): lax.all_to_all(outgoing, 'pts', split_axis=0, concat_axis=0, tiled=True)  23.9 us
    pallas_call x1, Pallas kernels, run_main(): pl.pallas_call(functools.partial(main_kernel, per_device=per_device, knbr...  9.32 us
    all_to_all x1, starting transfers between devices, shards(): lax.all_to_all(outgoing, 'pts', split_axis=0, concat_axis=0, tiled=True)  5.36 us
    ppermute x3, starting transfers between devices, shards(): lax.ppermute(pieces[d], 'pts', [(p, p ^ d) for p in range(n_pts)])  5.06 us
    pallas_call x1, Pallas kernels, shards(): pl.pallas_call(functools.partial(send_kernel, boxes=boxes, slots=slots, o...  3.47 us
  transfers between devices with their start and end apart: 4, of which 1 were waited for; matrix products, arithmetic and copies ran while one was open for 0% of the time, Pallas kernels for 0%

profile of v7, /device:TPU:1, one launch (start us, length us, event | category | flops | bytes accessed | tf_op | source)
XLA Modules:
  0.0 129.5 jit_solution(6570848113538189106)
XLA Ops:
  0.0 2.5 %shard_map.82 = (bf16[4,16,32,128]{3,2,1,0:T(8,128)(2,1)}, bf16[4,16,32,128]{3,2,1,0:T(8,128)(2,1)}, bf16[4,16,32,128]{3,2,1,0:T(8,128)(2,1)}, bf16[4,16,32,128]...) custom-call(bf16[4,16,128,128]{3,2,1,0:T(8,128)(2,1)} %density_ref.1, s32[4,16]{1,0:T(4,128)} %screen_hbm.1, ...), custom_call_target="tpu_custom_call" | custom-call | tf_op jit(solution)/shard_map/pallas_call | solution.py:329
  2.6 3.3 %collective-permute-start = (bf16[4,16,32,128]{3,2,1,0:T(8,128)(2,1)}, bf16[4,16,32,128]{3,2,1,0:T(8,128)(2,1)S(1)}, u32[]{:S(2)}, u32[]{:S(2)}) collective-permute-start(bf16[4,16,32,128]{3,2,1,0:T(8,128)(2,1)} %get-tuple-element.15), channel_id=1, source_target_pairs={{0,8},{8,0},{16,24},{24,16},{32,40},{40,32},{48,56},{56,48},{64,72... | collective-permute-start | bytes 1572872 | tf_op jit(solution)/shard_map/ppermute | solution.py:351
  5.9 0.0 collective-permute-start.1
  5.9 1.7 %collective-permute-start.2 = (bf16[4,16,32,128]{3,2,1,0:T(8,128)(2,1)}, bf16[4,16,32,128]{3,2,1,0:T(8,128)(2,1)S(1)}, u32[]{:S(2)}, u32[]{:S(2)}) collective-permute-start(bf16[4,16,32,128]{3,2,1,0:T(8,128)(2,1)} %get-tuple-element.17), channel_id=1, source_target_pairs={{0,24},{8,16},{16,8},{24,0},{32,56},{40,48},{48,40},{56,32},{64,88... | collective-permute-start | bytes 1572872 | tf_op jit(solution)/shard_map/ppermute | solution.py:351
  7.6 26.6 %all_to_all.15.lists_hbm = s32[32,1,64]{2,1,0:T(1,128)S(1)} all-to-all(s32[32,1,64]{2,1,0:T(1,128)S(1)} %get-tuple-element.13), channel_id=1, replica_groups=mesh['pts'=32,'bas'=8] {'pts'}, dimensions={0} | all-to-all | bytes 16384 | tf_op jit(solution)/shard_map/all_to_all | solution.py:353
  34.2 0.0 collective-permute-done.refs_1_
  34.2 0.0 collective-permute-done.1.refs_2_
  34.2 0.0 collective-permute-done.2.refs_3_
  34.2 3.5 %shard_map.83 = bf16[32,8,32,256]{3,2,1,0:T(8,128)(2,1)} custom-call(s32[32,1,64]{2,1,0:T(1,128)S(1)} %all_to_all.15.lists_hbm, bf16[4,16,32,128]{3,2,1,0:T(8,128)(2,1)} %get-tuple-element.14.refs_0_, bf16[4,16,32,128]{3,2,1,0:T(8,128)(2,1)S(1)} %collective-permute-done.refs_1_, bf16[4,16,32,128]{3,2,1,0:T(8,128)(2,1)S(1)} %collective-permute-done.1.refs_2_, ...), custom_call_target="tpu_custom_call" | custom-call | tf_op jit(solution)/shard_map/pallas_call | solution.py:369
  37.7 0.0 copy-start.3
  37.7 0.0 copy-start
  37.7 0.0 copy-start.2
  37.7 5.4 %all-to-all-start.1 = ((bf16[32,8,32,256]{3,2,1,0:T(8,128)(2,1)}), bf16[32,8,32,256]{3,2,1,0:T(8,128)(2,1)}, u32[]{:S(2)}, u32[]{:S(2)}) async-start(bf16[32,8,32,256]{3,2,1,0:T(8,128)(2,1)} %shard_map.83), calls=%async_computation.1 | async-start | bytes 8388608 | tf_op jit(solution)/shard_map/all_to_all | solution.py:384
  43.1 24.9 %all-gather = f32[512,128]{1,0:T(8,128)S(1)} all-gather(f32[64,128]{1,0:T(8,128)S(1)} %get-tuple-element.18), channel_id=2, replica_groups=mesh['pts'=32,'bas'=8] {'bas'}, dimensions={0}, use_global_device_ids=true | all-gather | bytes 294912 | tf_op jit(solution)/shard_map/all_gather | solution.py:368
  68.0 0.0 copy-done.3
  68.0 0.4 shard_map.84
  68.4 0.0 copy-start.1
  68.4 1.1 copy-done.1
  69.5 23.9 %all-to-all-done.1 = bf16[32,8,32,256]{3,2,1,0:T(8,128)(2,1)} async-done(((bf16[32,8,32,256]{3,2,1,0:T(8,128)(2,1)}), bf16[32,8,32,256]{3,2,1,0:T(8,128)(2,1)}, u32[]{:S(2)}, u32[]{:S(2)}) %all-to-all-start.1) | async-done | bytes 4194336 | tf_op jit(solution)/shard_map/all_to_all | solution.py:384
  93.5 0.0 copy-done
  93.5 0.0 copy-done.2
  93.5 9.3 %shard_map.85 = f32[256,128]{1,0:T(8,128)S(1)} custom-call(s32[4,16]{1,0:T(4,128)} %screen_hbm.1, bf16[4,448,2048]{2,1,0:T(8,128)(2,1)} %chi_ref.1, bf16[3,4,448,256]{3,2,1,0:T(8,128)(2,1)S(1)} %copy-done, bf16[8,4,8,32,256]{4,3,2,1,0:T(8,128)(2,1)} %bitcast.arrived_ref, f32[448,128]{1,0:T(8,128)S(1)} %get-tuple-element.19.weight_ref, ...), custom_call_target="tpu_custom_call" | custom-call | flops 2000000000 | bytes 30000000 | tf_op jit(solution)/shard_map/pallas_call | solution.py:286
  102.8 26.0 %all_to_all.16 = f32[256,1,36]{2,1,0:T(1,128)S(1)} all-to-all(f32[256,1,36]{2,1,0:T(1,128)S(1)} %bitcast.9), channel_id=1, replica_groups=mesh['pts'=32,'bas'=8] {'pts','bas'}, dimensions={0} | all-to-all | bytes 73728 | tf_op jit(solution)/shard_map/all_to_all | solution.py:399
  128.8 0.7 shard_map.86
Async XLA Ops:
  2.6 31.7 %collective-permute-start = (bf16[4,16,32,128]{3,2,1,0:T(8,128)(2,1)}, bf16[4,16,32,128]{3,2,1,0:T(8,128)(2,1)S(1)}, u32[]{:S(2)}, u32[]{:S(2)}) collective-permute-start(bf16[4,16,32,128]{3,2,1,0:T(8,128)(2,1)} %get-tuple-element.15), channel_id=1, source_target_pairs={{0,8},{8,0},{16,24},{24,16},{32,40},{40,32},{48,56},{56,48},{64,72... | collective-permute-start | bytes 1572872 | tf_op jit(solution)/shard_map/ppermute | solution.py:351
  5.9 28.3 %collective-permute-start.1 = (bf16[4,16,32,128]{3,2,1,0:T(8,128)(2,1)}, bf16[4,16,32,128]{3,2,1,0:T(8,128)(2,1)S(1)}, u32[]{:S(2)}, u32[]{:S(2)}) collective-permute-start(bf16[4,16,32,128]{3,2,1,0:T(8,128)(2,1)} %get-tuple-element.16), channel_id=1, source_target_pairs={{0,16},{8,24},{16,0},{24,8},{32,48},{40,56},{48,32},{56,40},{64,80... | collective-permute-start | bytes 1572872 | tf_op jit(solution)/shard_map/ppermute | solution.py:351
  5.9 28.3 %collective-permute-start.2 = (bf16[4,16,32,128]{3,2,1,0:T(8,128)(2,1)}, bf16[4,16,32,128]{3,2,1,0:T(8,128)(2,1)S(1)}, u32[]{:S(2)}, u32[]{:S(2)}) collective-permute-start(bf16[4,16,32,128]{3,2,1,0:T(8,128)(2,1)} %get-tuple-element.17), channel_id=1, source_target_pairs={{0,24},{8,16},{16,8},{24,0},{32,56},{40,48},{48,40},{56,32},{64,88... | collective-permute-start | bytes 1572872 | tf_op jit(solution)/shard_map/ppermute | solution.py:351
  37.7 30.3 %copy-start.3 = (f32[4,448]{1,0:T(4,128)S(1)}, f32[4,448]{1,0:T(4,128)}, u32[]{:S(2)}) copy-start(f32[4,448]{1,0:T(4,128)} %weight_ref.1) | copy-start | bytes 21508
  37.7 55.8 %copy-start = (bf16[3,4,448,256]{3,2,1,0:T(8,128)(2,1)S(1)}, bf16[3,4,448,256]{3,2,1,0:T(8,128)(2,1)}, u32[]{:S(2)}) copy-start(bf16[3,4,448,256]{3,2,1,0:T(8,128)(2,1)} %dchi_ref.1) | copy-start | bytes 8257540
  37.7 55.8 %copy-start.2 = (s32[2048]{0:T(1024)S(1)}, s32[2048]{0:T(1024)}, u32[]{:S(2)}) copy-start(s32[2048]{0:T(1024)} %param.13) | copy-start | bytes 24580
  37.7 55.7 %all-to-all-start.1 = ((bf16[32,8,32,256]{3,2,1,0:T(8,128)(2,1)}), bf16[32,8,32,256]{3,2,1,0:T(8,128)(2,1)}, u32[]{:S(2)}, u32[]{:S(2)}) async-start(bf16[32,8,32,256]{3,2,1,0:T(8,128)(2,1)} %shard_map.83), calls=%async_computation.1 | async-start | bytes 8388608 | tf_op jit(solution)/shard_map/all_to_all | solution.py:384
  68.4 1.2 copy-start.1
